TPU v7x, 32 devices: a whole 2x2x4 slice. The times are simulated.
32 devices in a mesh: dp: 4 (over z), own: 8 (over y, x, core).
Axes of the slice: x: 2, y: 2, z: 4, core: 2. Of those that a mesh axis runs over, the one named last changes fastest.
Arguments:
- inputs: bfloat16 [1024, 8192], P('dp', 'own'), may hold values from -6 to 6
- out_grad: bfloat16 [1024, 8192], P('dp', 'own'), may hold values from -6 to 6
- int_values: bfloat16 [3, 3328, 128, 128], P(None, 'own'), may hold values from -127 to 127, as said below
- scales: float32 [3, 3328], P(None, 'own'), may hold values from 0.00011792096 to 0.0004684968
- block_rows: int32 [3, 128, 26], replicated, may hold values from 0 to 63, as said below
- holder: int32 [3, 128, 26], replicated, may hold values from 0 to 7, as said below
- slot_index: int32 [3, 128, 26], replicated, may hold values from 0 to 415, as said below
Outputs:
- input_grad: bfloat16 [1024, 8192], P('dp', 'own')
- grad_weights: bfloat16 [3, 3328, 128, 128], P(None, 'own', 'dp')
Inputs may be any that keep to these rules, and one draw needn't show every extreme that they name: int_values holds whole numbers. `block_rows`: the 26 row blocks of each block column of each matrix are distinct and increasing. For each matrix and each group of 16 consecutive block columns, no holder holds more than 70 of the group's blocks, and some holder holds exactly 70; each holder holds exactly 416 blocks of each matrix. For each matrix the pairs (holder, slot_index) are distinct, so every slot of every holder holds one block.
All inputs are finite; a program needn't handle non-finite values.
Results may differ from a plain program's by a relative error of at most 0.015.
Values may be sent and summed in bfloat16 or wider, within the bound.
No kernel may reach another device: no remote copies, remote signals or barrier semaphores. Data moves between devices by JAX's collectives and lax.ppermute only.
A program may use at most 512 MiB of HBM per device.

v0:
```python
import functools
import math

import jax
import jax.numpy as jnp
from jax import lax
from jax.experimental import pallas as pl
from jax.experimental.pallas import tpu as pltpu
from jax.sharding import PartitionSpec as P

F32 = jnp.float32
BF16 = jnp.bfloat16
NT = (((1,), (1,)), ((), ()))
COST = pl.CostEstimate(flops=1024, bytes_accessed=1024, transcendentals=0)
PARAMS = pltpu.CompilerParams(vmem_limit_bytes=56 * 2**20)


def whole(shape):
    return pl.BlockSpec(shape, lambda *_: (0,) * len(shape))


def waiting(after):
    return [pl.BlockSpec(memory_space=pl.ANY)] * len(after)


def mark(value):
    return value.reshape((-1,) + value.shape[-2:])[0, :16, :128]


def tie(value, *after):
    def kernel(*refs):
        pass

    return pl.pallas_call(
        kernel,
        out_shape=jax.ShapeDtypeStruct(value.shape, value.dtype),
        in_specs=waiting((value,) + after),
        out_specs=pl.BlockSpec(memory_space=pl.ANY),
        input_output_aliases={0: 0},
        compiler_params=PARAMS,
        name="tie",
    )(value, *after)


def pack(which, ints, scales, slots, quarter, rows_each, after=()):
    slot_count, block = ints.shape[1], ints.shape[2]
    places = slots.shape[0]

    def kernel(slots, quarter, scales, ints, *refs):
        out = refs[-1]

        def place(index, _):
            slot = slots[index]
            out[index] = (ints[0, slot].astype(F32) * scales[slot]).astype(BF16)
            return _

        lax.fori_loop(0, places, place, 0, unroll=8)

    return pl.pallas_call(
        kernel,
        out_shape=jax.ShapeDtypeStruct((places, rows_each, block), BF16),
        grid_spec=pltpu.PrefetchScalarGridSpec(
            num_scalar_prefetch=3,
            grid=(1,),
            in_specs=[
                pl.BlockSpec(
                    (1, slot_count, rows_each, block), lambda g, s, q, c: (which, 0, q[0], 0)
                )
            ]
            + waiting(after),
            out_specs=whole((places, rows_each, block)),
        ),
        compiler_params=PARAMS,
        cost_estimate=COST,
        name="pack",
    )(slots, quarter, scales, ints, *after)


def forward(x, arrived, flat, rows, columns, row_blocks, after=()):
    places, rows_each, block = arrived.shape
    tokens, depth = x.shape
    keep = flat.shape[0] // columns
    quarters = block // rows_each

    def kernel(flat, rows, x, arrived, *refs):
        dense, out = refs[-2:]
        step = pl.program_id(0)
        dense[...] = jnp.zeros_like(dense)
        for half in range(2):
            base = (step * 2 + half) * keep
            lanes = slice(half * block, (half + 1) * block)

            def place(k, _):
                dense[rows[base + k], :, lanes] = arrived[flat[base + k]]
                return _

            lax.fori_loop(0, keep, place, 0, unroll=2)
        weights = dense[...].reshape(depth, 2 * block)
        result = jnp.dot(x[...], weights, preferred_element_type=F32)
        turned = jnp.transpose(result).astype(BF16)
        for half in range(2):
            for q in range(quarters):
                first = half * block + q * rows_each
                out[q, half] = turned[first : first + rows_each]

    return pl.pallas_call(
        kernel,
        out_shape=(
            jax.ShapeDtypeStruct((row_blocks, rows_each, columns * block), BF16),
            jax.ShapeDtypeStruct((quarters, columns, rows_each, tokens), BF16),
        ),
        grid_spec=pltpu.PrefetchScalarGridSpec(
            num_scalar_prefetch=2,
            grid=(columns // 2,),
            in_specs=[whole((tokens, depth)), whole((places, rows_each, block))] + waiting(after),
            out_specs=(
                pl.BlockSpec((row_blocks, rows_each, 2 * block), lambda g, f, r: (0, 0, g)),
                pl.BlockSpec((quarters, 2, rows_each, tokens), lambda g, f, r: (0, g, 0, 0)),
            ),
        ),
        compiler_params=PARAMS,
        cost_estimate=COST,
        name="forward",
    )(flat, rows, x, arrived, *after)


def forward_down(cotangents, arrived, flat, rows, quarter, first, columns, row_blocks):
    (near, far), _ = cotangents
    chips, tokens, width = near.shape
    planes = far.shape[1] + 1
    owners = 2 * chips
    places, rows_each, block = arrived.shape
    keep = flat.shape[0] // columns
    hidden = columns * rows_each
    per_owner = row_blocks // owners

    def kernel(flat, rows, quarter, first, near, far, near_other, far_other, arrived, out, dense):
        step = pl.program_id(0)

        @pl.when(step == 0)
        def _():
            dense[...] = jnp.zeros_like(dense)
            out[...] = jnp.zeros_like(out)
            for c in range(columns):

                def place(k, _):
                    row = rows[c * keep + k]
                    lane = pl.multiple_of((row % per_owner) * block, block)
                    dense[row // per_owner, c * rows_each : (c + 1) * rows_each, pl.ds(lane, block)] = (
                        arrived[flat[c * keep + k]]
                    )
                    return _

                lax.fori_loop(0, keep, place, 0, unroll=2)

        for core, (own, others) in enumerate(((near, far), (near_other, far_other))):
            weights = dense[2 * step + lax.rem(first[0] + core, 2)]
            for shift in range(planes):
                cotangent = own[0] if shift == 0 else others[0, shift - 1]
                plane = lax.rem(quarter[0] + planes - shift, planes)
                lanes = pl.ds(pl.multiple_of(plane * tokens, tokens), tokens)
                out[:, lanes] += lax.dot_general(
                    weights, cotangent, NT, preferred_element_type=F32
                )

    share = [
        pl.BlockSpec((1, tokens, width), lambda g, *_: (g, 0, 0)),
        pl.BlockSpec((1, planes - 1, tokens, width), lambda g, *_: (g, 0, 0, 0)),
    ]
    return pl.pallas_call(
        kernel,
        out_shape=jax.ShapeDtypeStruct((hidden, planes * tokens), F32),
        grid_spec=pltpu.PrefetchScalarGridSpec(
            num_scalar_prefetch=4,
            grid=(chips,),
            in_specs=share + share + [whole((places, rows_each, block))],
            out_specs=whole((hidden, planes * tokens)),
            scratch_shapes=[pltpu.VMEM((owners, hidden, width), BF16)],
        ),
        compiler_params=PARAMS,
        cost_estimate=COST,
        name="forward_down",
    )(flat, rows, quarter, first, *cotangents[0], *cotangents[1], arrived)


def weight_grad(x_turned, grad, flat, rows, places, row_blocks, factor, after=()):
    quarters, columns, rows_each, tokens = grad.shape
    depth = x_turned.shape[0]
    block = quarters * rows_each
    keep = flat.shape[0] // columns

    def kernel(flat, rows, x_turned, grad, *refs):
        out, natural, result = refs[-3:]
        step = pl.program_id(0)
        for half in range(2):
            for q in range(quarters):
                natural[half, q] = grad[q, half]
        right = natural[...].reshape(2 * block, tokens)
        product = lax.dot_general(x_turned[...], right, NT, preferred_element_type=F32)
        result[...] = (product * factor).astype(BF16).reshape(result.shape)
        for half in range(2):
            base = (step * 2 + half) * keep
            lanes = slice(half * block, (half + 1) * block)

            def place(k, _):
                out[flat[base + k]] = result[rows[base + k], :, lanes]
                return _

            lax.fori_loop(0, keep, place, 0, unroll=2)

    return pl.pallas_call(
        kernel,
        out_shape=(
            jax.ShapeDtypeStruct((places, rows_each, block), BF16),
            jax.ShapeDtypeStruct((columns, quarters, rows_each, tokens), BF16),
        ),
        grid_spec=pltpu.PrefetchScalarGridSpec(
            num_scalar_prefetch=2,
            grid=(columns // 2,),
            in_specs=[
                whole((depth, tokens)),
                pl.BlockSpec((quarters, 2, rows_each, tokens), lambda g, f, r: (0, g, 0, 0)),
            ]
            + waiting(after),
            out_specs=(
                whole((places, rows_each, block)),
                pl.BlockSpec((2, quarters, rows_each, tokens), lambda g, f, r: (g, 0, 0, 0)),
            ),
            scratch_shapes=[pltpu.VMEM((row_blocks, rows_each, 2 * block), BF16)],
        ),
        compiler_params=PARAMS,
        cost_estimate=COST,
        name="weight_grad",
    )(flat, rows, x_turned, grad, *after)


def weight_grad_down(
    value, cotangents, flat, rows, quarter, first, places, block, columns, row_blocks, factor
):
    (near, far), _ = cotangents
    chips, tokens, width = near.shape
    planes = far.shape[1] + 1
    owners = 2 * chips
    hidden = value.shape[0]
    rows_each = hidden // columns
    keep = flat.shape[0] // columns
    per_owner = row_blocks // owners

    def kernel(
        flat, rows, quarter, first, value, near, far, near_other, far_other, out, joined, result
    ):
        step = pl.program_id(0)
        for core, (own, others) in enumerate(((near, far), (near_other, far_other))):
            for shift in range(planes):
                cotangent = own[0] if shift == 0 else others[0, shift - 1]
                joined[lax.rem(quarter[0] + planes - shift, planes)] = cotangent
            right = joined[...].reshape(planes * tokens, width)
            product = jnp.dot(value[...], right, preferred_element_type=F32)
            result[2 * step + lax.rem(first[0] + core, 2)] = (product * factor).astype(BF16)

        @pl.when(step == chips - 1)
        def _():
            for c in range(columns):

                def place(k, _):
                    row = rows[c * keep + k]
                    lane = pl.multiple_of((row % per_owner) * block, block)
                    out[flat[c * keep + k]] = result[
                        row // per_owner, c * rows_each : (c + 1) * rows_each, pl.ds(lane, block)
                    ]
                    return _

                lax.fori_loop(0, keep, place, 0, unroll=2)

    share = [
        pl.BlockSpec((1, tokens, width), lambda g, *_: (g, 0, 0)),
        pl.BlockSpec((1, planes - 1, tokens, width), lambda g, *_: (g, 0, 0, 0)),
    ]
    return pl.pallas_call(
        kernel,
        out_shape=jax.ShapeDtypeStruct((places, rows_each, block), BF16),
        grid_spec=pltpu.PrefetchScalarGridSpec(
            num_scalar_prefetch=4,
            grid=(chips,),
            in_specs=[whole((hidden, planes * tokens))] + share + share,
            out_specs=whole((places, rows_each, block)),
            scratch_shapes=[
                pltpu.VMEM((planes, tokens, width), BF16),
                pltpu.VMEM((owners, hidden, width), BF16),
            ],
        ),
        compiler_params=PARAMS,
        cost_estimate=COST,
        name="weight_grad_down",
    )(flat, rows, quarter, first, value, *cotangents[0], *cotangents[1])


def input_part(weights, grad, first, chips, earlier=()):
    depth, units = weights.shape
    tokens = grad.shape[1]
    rows = depth // (2 * chips)

    def kernel(first, left, right, grad, *refs):
        earlier, outs = refs[:-2], refs[-2:]
        both = jnp.concatenate([left[...], right[...]], axis=0)
        product = jnp.dot(both, grad[...], preferred_element_type=F32)
        for core in range(2):
            part = product[core * rows : (core + 1) * rows]
            if earlier:
                part = earlier[core][0] + part
            outs[core][0] = part.astype(outs[core].dtype)

    share = pl.BlockSpec((1, rows, tokens), lambda g, f: (g, 0, 0))
    out = jax.ShapeDtypeStruct((chips, rows, tokens), BF16 if earlier else F32)
    return pl.pallas_call(
        kernel,
        out_shape=(out, out),
        grid_spec=pltpu.PrefetchScalarGridSpec(
            num_scalar_prefetch=1,
            grid=(chips,),
            in_specs=[
                pl.BlockSpec((rows, units), lambda g, f: (2 * g + f[0], 0)),
                pl.BlockSpec((rows, units), lambda g, f: (2 * g + 1 - f[0], 0)),
                whole((units, tokens)),
            ]
            + [share] * len(earlier),
            out_specs=(share, share),
        ),
        compiler_params=PARAMS,
        cost_estimate=COST,
        name="input_part",
    )(first, weights, weights, grad, *earlier)


def unpack(which, returned, source, total):
    places, rows_each, block = returned.shape
    slot_count = source.shape[0]

    def kernel(source, returned, *refs):
        out = refs[-1]

        def place(slot, _):
            out[0, slot] = returned[source[slot]]
            return _

        lax.fori_loop(0, slot_count, place, 0, unroll=8)

    shape = (3, slot_count, rows_each, block)
    extra = [] if total is None else [total]
    return pl.pallas_call(
        kernel,
        out_shape=jax.ShapeDtypeStruct(shape, BF16),
        grid_spec=pltpu.PrefetchScalarGridSpec(
            num_scalar_prefetch=1,
            grid=(1,),
            in_specs=[whole((places, rows_each, block))] + waiting(extra),
            out_specs=pl.BlockSpec((1,) + shape[1:], lambda g, s: (which, 0, 0, 0)),
        ),
        input_output_aliases={2: 0} if extra else {},
        compiler_params=PARAMS,
        cost_estimate=COST,
        name="unpack",
    )(source, returned, *extra)


def in_order(kept, quarter, after=()):
    count, shape = len(kept), kept[0].shape

    def kernel(quarter, *refs):
        for shift in range(count):
            refs[-1][lax.rem(quarter[0] + count - shift, count)] = refs[shift][...]

    return pl.pallas_call(
        kernel,
        out_shape=jax.ShapeDtypeStruct((count,) + shape, kept[0].dtype),
        grid_spec=pltpu.PrefetchScalarGridSpec(
            num_scalar_prefetch=1,
            grid=(1,),
            in_specs=[whole(shape)] * count + waiting(after),
            out_specs=whole((count,) + shape),
        ),
        compiler_params=PARAMS,
        cost_estimate=COST,
        name="in_order",
    )(quarter, *kept, *after)


def silu_parts(gate, up_value, grad_act):
    sigmoid_g = jax.nn.sigmoid(gate)
    activated = gate * sigmoid_g
    value = (activated * up_value).astype(BF16)
    grad_gate = (grad_act * up_value * sigmoid_g * (1.0 + gate * (1.0 - sigmoid_g))).astype(BF16)
    grad_up = (grad_act * activated).astype(BF16)
    return (value, grad_gate, grad_up)


def per_device(inputs, out_grad, int_values, scales, block_rows, holder, slot_index):
    own_count = lax.axis_size("own")
    data_count = lax.axis_size("dp")
    own_index = lax.axis_index("own")
    data_index = lax.axis_index("dp")
    local_tokens, local_width = inputs.shape
    tokens = local_tokens * data_count
    slot_count = int_values.shape[1]
    block = int_values.shape[2]
    keep = block_rows.shape[2]
    width = local_width * own_count
    row_blocks = width // block
    columns = block_rows.shape[1] // own_count
    group = columns * keep
    active = 3 * own_count // 4
    capacity = (group + active - 1) // active
    places = own_count * capacity
    rows_each = block // data_count
    depth = row_blocks * rows_each
    hidden = columns * rows_each
    factor = 1.0 / math.sqrt(tokens)

    holder_group = holder.reshape(3, own_count, group)
    slot_group = slot_index.reshape(3, own_count, group)
    mine = (holder_group == own_index).astype(jnp.int32)
    rank = jnp.cumsum(mine, axis=2) - 1
    spots = jnp.arange(capacity, dtype=jnp.int32)
    picked = (mine[..., None] == 1) & (rank[..., None] == spots)
    bucket_slot = jnp.sum(jnp.where(picked, slot_group[..., None], 0), axis=2)
    used = spots < jnp.sum(mine, axis=2)[..., None]
    hits = used[..., None] & (bucket_slot[..., None] == jnp.arange(slot_count, dtype=jnp.int32))
    bucket_index = jnp.arange(places, dtype=jnp.int32).reshape(own_count, capacity)
    source = jnp.sum(jnp.where(hits, bucket_index[None, :, :, None], 0), axis=(1, 2))
    bucket_slot = bucket_slot.reshape(3, places)
    own_holder = lax.dynamic_index_in_dim(holder_group, own_index, 1, keepdims=False)
    entries = jnp.arange(group, dtype=jnp.int32)
    earlier = (own_holder[:, :, None] == own_holder[:, None, :]) & (
        entries[None, :, None] < entries[None, None, :]
    )
    position = jnp.sum(earlier.astype(jnp.int32), axis=1)
    flat = own_holder * capacity + position
    rows = lax.dynamic_index_in_dim(
        block_rows.reshape(3, own_count, group), own_index, 1, keepdims=False
    )
    quarter = data_index.astype(jnp.int32).reshape(1)

    def exchange(parts):
        kept = [parts[0]]
        for s in range(1, data_count):
            turn = [(i, (i + s) % data_count) for i in range(data_count)]
            kept.append(lax.ppermute(parts[s], "dp", turn))
        return kept

    def send(which, after=()):
        sending = pack(
            which, int_values, scales[which], bucket_slot[which], quarter, rows_each, after
        )
        return sending.reshape(own_count, capacity, rows_each, block)

    def receive(sending):
        arrived = lax.all_to_all(sending, "own", split_axis=0, concat_axis=0, tiled=True)
        return arrived.reshape(places, rows_each, block)

    chips = own_count // 2
    likes = [[core + 2 * chip for chip in range(chips)] for core in range(2)]
    swap = [(i, i ^ 1) for i in range(own_count)]
    core = jnp.remainder(own_index, 2).astype(jnp.int32).reshape(1)

    near = lax.all_gather(out_grad, "own", axis=0, axis_index_groups=likes)

    local = inputs.reshape(local_tokens, row_blocks // own_count, data_count, rows_each)
    local = local.transpose(2, 0, 1, 3).reshape(data_count, local_tokens, depth // own_count)
    twice = jnp.concatenate([local, local])
    local = exchange(
        [lax.dynamic_index_in_dim(twice, data_index + s, 0, keepdims=False) for s in range(data_count)]
    )
    local = in_order(local, quarter, (mark(near),))
    gathered = lax.all_gather(local.reshape(tokens, depth // own_count), "own", axis=0)
    sending_gate, sending_up, sending_down = send(0), send(1, (mark(local),)), send(2, (mark(local),))
    arrived_gate = receive(sending_gate)

    far = tie(jnp.stack(exchange([out_grad] * data_count)[1:]), mark(arrived_gate))
    far = lax.all_gather(far, "own", axis=0, axis_index_groups=likes)

    x = gathered.transpose(1, 0, 2).reshape(tokens, depth)
    x_turned = gathered.transpose(0, 2, 1).reshape(depth, tokens)
    packed = (mark(sending_up), mark(sending_down))
    gate_weights, part = forward(x, arrived_gate, flat[0], rows[0], columns, row_blocks, packed)
    gate = lax.psum_scatter(part, "dp", scatter_dimension=0)
    arrived_up = receive(tie(sending_up, mark(gate_weights)))
    up_weights, part = forward(x, arrived_up, flat[1], rows[1], columns, row_blocks)
    up_value = lax.psum_scatter(part, "dp", scatter_dimension=0)
    far = tie(far, mark(up_weights))
    cotangents = ((near, far), (lax.ppermute(near, "own", swap), lax.ppermute(far, "own", swap)))
    arrived_down = receive(tie(sending_down, mark(up_weights)))
    grad_act = forward_down(
        cotangents, arrived_down, flat[2], rows[2], quarter, core, columns, row_blocks
    )
    value, grad_gate, grad_up = silu_parts(
        gate.reshape(hidden, tokens).astype(F32), up_value.reshape(hidden, tokens).astype(F32), grad_act
    )
    shape = (columns, rows_each, tokens)

    def give_back(leaving):
        leaving = leaving.reshape(own_count, capacity, rows_each, block)
        returned = lax.all_to_all(leaving, "own", split_axis=0, concat_axis=0, tiled=True)
        return returned.reshape(places, rows_each, block)

    def natural(grad):
        return grad.reshape(columns * block, tokens)

    all_up = lax.all_gather(grad_up.reshape(shape), "dp", axis=0)
    leaving = weight_grad_down(
        value, cotangents, flat[2], rows[2], quarter, core, places, block, columns, row_blocks, factor
    )
    all_gate = lax.all_gather(grad_gate.reshape(shape), "dp", axis=0)
    returned = give_back(leaving)
    leaving, whole_up = weight_grad(
        x_turned, all_up, flat[1], rows[1], places, row_blocks, factor, (mark(returned),)
    )
    total = unpack(2, returned, source[2], None)
    returned = give_back(leaving)
    up_weights = up_weights.reshape(depth, columns * block)
    back = input_part(up_weights, natural(whole_up), core, chips)
    leaving, whole_gate = weight_grad(
        x_turned,
        all_gate,
        flat[0],
        rows[0],
        places,
        row_blocks,
        factor,
        (mark(returned), mark(back[0]), mark(total)),
    )
    total = unpack(1, returned, source[1], total)
    returned = give_back(leaving)

    gate_weights = gate_weights.reshape(depth, columns * block)
    back = input_part(gate_weights, natural(whole_gate), core, chips, back)
    back = back[0].astype(F32) + lax.ppermute(back[1], "own", swap).astype(F32)
    back = lax.psum_scatter(
        back.astype(BF16), "own", scatter_dimension=0, axis_index_groups=likes
    )
    back = back.reshape(depth // own_count, data_count, local_tokens).transpose(1, 0, 2)
    back = lax.all_to_all(back, "dp", split_axis=0, concat_axis=0, tiled=True)
    back = back.reshape(data_count, row_blocks // own_count, rows_each, local_tokens)
    input_grad = back.transpose(3, 1, 0, 2).reshape(local_tokens, local_width)
    total = unpack(0, returned, source[0], total)
    return (input_grad, total)


def solution(mesh):
    placed = (
        P("dp", "own"),
        P("dp", "own"),
        P(None, "own", None, None),
        P(None, "own"),
        P(),
        P(),
        P(),
    )
    return jax.shard_map(
        per_device,
        mesh=mesh,
        in_specs=placed,
        out_specs=(P("dp", "own"), P(None, "own", "dp", None)),
        check_vma=False,
    )
```

profile of v0, /device:TPU:0, one launch (start us, length us, event | category | flops | bytes accessed | tf_op | source)
XLA Modules:
  0.0 708.6 jit_solution(7408166567083686316)
XLA Ops:
  8.0 1.2 copy.90
  9.6 3.1 collective-permute-start
  12.8 2.7 collective-permute-start.1
  15.5 1.4 collective-permute-start.2
  17.7 30.2 %all-gather.14.cloned.1.call-done = bf16[1024,1024]{1,0:T(8,128)(2,1)} async-done(((bf16[256,1024]{1,0:T(8,128)(2,1)}), bf16[1024,1024]{1,0:T(8,128)(2,1)}) %all-gather.14.cloned.1.call-update) | async-done | bytes 2097168 | tf_op jit(solution)/shard_map/all_gather | solution.py:465
  47.9 1.3 slice_bitcast_fusion.8.refs_4_
  49.9 1.9 in_order.1
  52.5 3.4 reduce-window.6
  56.4 3.6 select_reduce_fusion.1
  61.4 6.2 pack.3
  67.5 4.8 all-to-all-start
  72.4 1.5 collective-permute-start.3
  73.9 2.3 collective-permute-start.5
  76.9 12.2 %collective-permute-done.3 = bf16[256,1024]{1,0:T(8,128)(2,1)S(1)} collective-permute-done((bf16[256,1024]{1,0:T(8,128)(2,1)S(1)}, bf16[256,1024]{1,0:T(8,128)(2,1)S(1)}, u32[]{:S(2)}, u32[]{:S(2)}) %collective-permute-start.3) | collective-permute-done | bytes 524320 | tf_op jit(solution)/shard_map/ppermute | solution.py:447
  89.0 10.0 %collective-permute-done.5 = bf16[256,1024]{1,0:T(8,128)(2,1)S(1)} collective-permute-done((bf16[256,1024]{1,0:T(8,128)(2,1)S(1)}, bf16[256,1024]{1,0:T(8,128)(2,1)S(1)}, u32[]{:S(2)}, u32[]{:S(2)}) %collective-permute-start.5) | collective-permute-done | bytes 524320 | tf_op jit(solution)/shard_map/ppermute | solution.py:447
  99.0 23.1 %collective-permute-done.4 = bf16[256,1024]{1,0:T(8,128)(2,1)S(1)} collective-permute-done((bf16[256,1024]{1,0:T(8,128)(2,1)S(1)}, bf16[256,1024]{1,0:T(8,128)(2,1)S(1)}, u32[]{:S(2)}, u32[]{:S(2)}) %collective-permute-start.4) | collective-permute-done | bytes 524320 | tf_op jit(solution)/shard_map/ppermute | solution.py:447
  122.1 1.3 pad_maximum_fusion.refs_0_
  123.4 13.5 %all-to-all-done = bf16[8,70,32,128]{3,2,1,0:T(8,128)(2,1)} async-done(((bf16[8,70,32,128]{3,2,1,0:T(8,128)(2,1)}), bf16[8,70,32,128]{3,2,1,0:T(8,128)(2,1)}, u32[]{:S(2)}, u32[]{:S(2)}) %all-to-all-start) | async-done | bytes 4587552 | tf_op jit(solution)/shard_map/all_to_all | solution.py:457
  136.9 1.3 slice_bitcast_fusion.4.refs_1_
  141.8 1.3 slice_bitcast_fusion.7.refs_0_
  143.1 6.8 pack.5
  149.8 6.2 pack.4
  156.1 1.3 slice_bitcast_fusion.5
  157.4 4.7 copy.107
  162.1 18.7 %forward.2 = (bf16[64,32,2048]{2,1,0:T(8,128)(2,1)}, bf16[4,16,32,1024]{3,2,1,0:T(8,128)(2,1)}) custom-call(s32[416]{0:T(512)} %bitcast.151, s32[416]{0:T(512)} %bitcast.147, bf16[1024,2048]{1,0:T(8,128)(2,1)} %bitcast.107, bf16[560,32,128]{2,1,0:T(8,128)(2,1)} %bitcast.19.arrived, bf16[16,128]{1,0:T(8,128)(2,1)} %get-tuple-element.63.refs_0_, ...), custom_call_target="tpu_custom_call" | custom-call | flops 1024 | bytes 1024 | tf_op jit(solution)/shard_map/forward/pallas_call | solution.py:106
  180.9 1.3 slice_bitcast_fusion.10.refs_1_
  182.1 75.3 %all_to_all.35 = bf16[8,70,32,128]{3,2,1,0:T(8,128)(2,1)} all-to-all(bf16[8,70,32,128]{3,2,1,0:T(8,128)(2,1)} %tie.5), channel_id=1, replica_groups=mesh['dp'=4,'own'=8] {'own'}, dimensions={0} | all-to-all | bytes 9175040 | tf_op jit(solution)/shard_map/all_to_all | solution.py:457
  257.4 18.8 %forward.3 = (bf16[64,32,2048]{2,1,0:T(8,128)(2,1)}, bf16[4,16,32,1024]{3,2,1,0:T(8,128)(2,1)}) custom-call(s32[416]{0:T(512)} %bitcast.153, s32[416]{0:T(512)} %bitcast.149, bf16[1024,2048]{1,0:T(8,128)(2,1)} %bitcast.108, bf16[560,32,128]{2,1,0:T(8,128)(2,1)} %bitcast.117), custom_call_target="tpu_custom_call" | custom-call | flops 1024 | bytes 1024 | tf_op jit(solution)/shard_map/forward/pallas_call | solution.py:106
  276.2 1.3 slice_bitcast_fusion.9.refs_1_
  277.5 4.8 all-to-all-start.2
  283.0 8.6 %collective-permute-done.6.near_other = bf16[4,256,1024]{2,1,0:T(8,128)(2,1)} collective-permute-done((bf16[4,256,1024]{2,1,0:T(8,128)(2,1)S(1)}, bf16[4,256,1024]{2,1,0:T(8,128)(2,1)}, u32[]{:S(2)}, u32[]{:S(2)}) %collective-permute-start.6) | collective-permute-done | bytes 2097184 | tf_op jit(solution)/shard_map/ppermute | solution.py:490
  291.6 44.0 %all-to-all-done.2 = bf16[8,70,32,128]{3,2,1,0:T(8,128)(2,1)} async-done(((bf16[8,70,32,128]{3,2,1,0:T(8,128)(2,1)}), bf16[8,70,32,128]{3,2,1,0:T(8,128)(2,1)}, u32[]{:S(2)}, u32[]{:S(2)}) %all-to-all-start.2) | async-done | bytes 4587552 | tf_op jit(solution)/shard_map/all_to_all | solution.py:457
  335.6 23.8 %forward_down.1 = f32[512,1024]{1,0:T(8,128)} custom-call(s32[416]{0:T(512)} %bitcast.145, s32[416]{0:T(512)} %bitcast.143, s32[1]{0:T(128)} %bitcast.3.quarter, s32[1]{0:T(128)} %bitcast.first, bf16[4,256,1024]{2,1,0:T(8,128)(2,1)} %bitcast.121, bf16[4,3,256,1024]{3,2,1,0:T(8,128)(2,1)} %tie.6.far, bf16[4,256,1024]{2,1,0:T(8,128)(2,1)} %collective-permute-done.6.near_other, ...), custom_call_target="tpu_custom_call" | custom-call | flops 1024 | bytes 1024 | tf_op jit(solution)/shard_map/forward_down/pallas_call | solution.py:170
  359.4 42.7 %reduce-scatter.6.cloned.1.call-done = bf16[1,16,32,1024]{3,2,1,0:T(8,128)(2,1)} async-done(((bf16[4,16,32,1024]{3,2,1,0:T(8,128)(2,1)}), bf16[1,16,32,1024]{3,2,1,0:T(8,128)(2,1)}) %reduce-scatter.6.cloned.1.call-update) | async-done | bytes 1048592 | tf_op jit(solution)/shard_map/reduce_scatter | solution.py:488
  402.1 5.5 multiply_convert_fusion
  407.6 20.7 %weight_grad_down.1 = bf16[560,32,128]{2,1,0:T(8,128)(2,1)} custom-call(s32[416]{0:T(512)} %bitcast.146, s32[416]{0:T(512)} %bitcast.144, s32[1]{0:T(128)} %bitcast.3.quarter, s32[1]{0:T(128)} %bitcast.first, bf16[512,1024]{1,0:T(8,128)(2,1)} %get-tuple-element.42.value, bf16[4,256,1024]{2,1,0:T(8,128)(2,1)} %bitcast.122, bf16[4,3,256,1024]{3,2,1,0:T(8,128)(2,1)} %tie.6.far, ...), custom_call_target="tpu_custom_call" | custom-call | flops 1024 | bytes 1024 | tf_op jit(solution)/shard_map/weight_grad_down/pallas_call | solution.py:279
  428.2 4.6 all-to-all-start.3
  433.6 6.5 copy.101
  440.1 46.1 %all-to-all-done.3 = bf16[8,70,32,128]{3,2,1,0:T(8,128)(2,1)} async-done(((bf16[8,70,32,128]{3,2,1,0:T(8,128)(2,1)}), bf16[8,70,32,128]{3,2,1,0:T(8,128)(2,1)}, u32[]{:S(2)}, u32[]{:S(2)}) %all-to-all-start.3) | async-done | bytes 4587552 | tf_op jit(solution)/shard_map/all_to_all | solution.py:502
  486.2 1.3 slice_bitcast_fusion.3.refs_0_
  487.5 1.5 all-gather.12.cloned.1.call-done.grad
  489.0 18.2 %weight_grad.2 = (bf16[560,32,128]{2,1,0:T(8,128)(2,1)}, bf16[16,4,32,1024]{3,2,1,0:T(8,128)(2,1)}) custom-call(s32[416]{0:T(512)} %bitcast.154, s32[416]{0:T(512)} %bitcast.150, bf16[2048,1024]{1,0:T(8,128)(2,1)} %bitcast.109, bf16[4,16,32,1024]{3,2,1,0:T(8,128)(2,1)} %all-gather.12.cloned.1.call-done.grad, bf16[16,128]{1,0:T(8,128)(2,1)} %slice_bitcast_fusion.3.refs_0_), custom_call_target="tpu_custom_call" | custom-call | flops 1024 | bytes 1024 | tf_op jit(solution)/shard_map/weight_grad/pallas_call | solution.py:211
  507.2 4.6 all-to-all-start.4
  512.4 1.0 select_reduce_fusion
  513.9 5.5 unpack.3.refs_0_
  519.4 1.3 slice_bitcast_fusion.1.refs_2_
  520.7 13.6 %input_part.2 = (f32[4,256,1024]{2,1,0:T(8,128)}, f32[4,256,1024]{2,1,0:T(8,128)}) custom-call(s32[1]{0:T(128)} %bitcast.first, bf16[2048,2048]{1,0:T(8,128)(2,1)} %bitcast.111, bf16[2048,2048]{1,0:T(8,128)(2,1)} %bitcast.112, bf16[2048,1024]{1,0:T(8,128)(2,1)} %bitcast.128), custom_call_target="tpu_custom_call" | custom-call | flops 1024 | bytes 1024 | tf_op jit(solution)/shard_map/input_part/pallas_call | solution.py:315
  534.3 1.3 slice_bitcast_fusion.refs_1_
  535.6 29.5 %all-to-all-done.4 = bf16[8,70,32,128]{3,2,1,0:T(8,128)(2,1)} async-done(((bf16[8,70,32,128]{3,2,1,0:T(8,128)(2,1)}), bf16[8,70,32,128]{3,2,1,0:T(8,128)(2,1)}, u32[]{:S(2)}, u32[]{:S(2)}) %all-to-all-start.4) | async-done | bytes 4587552 | tf_op jit(solution)/shard_map/all_to_all | solution.py:502
  565.1 1.3 slice_bitcast_fusion.2.refs_0_
  566.4 3.5 all-gather.10.cloned.1.call-done.grad
  569.9 18.4 %weight_grad.3 = (bf16[560,32,128]{2,1,0:T(8,128)(2,1)}, bf16[16,4,32,1024]{3,2,1,0:T(8,128)(2,1)}) custom-call(s32[416]{0:T(512)} %bitcast.152, s32[416]{0:T(512)} %bitcast.148, bf16[2048,1024]{1,0:T(8,128)(2,1)} %bitcast.110, bf16[4,16,32,1024]{3,2,1,0:T(8,128)(2,1)} %all-gather.10.cloned.1.call-done.grad, bf16[16,128]{1,0:T(8,128)(2,1)} %slice_bitcast_fusion.2.refs_0_, ...), custom_call_target="tpu_custom_call" | custom-call | flops 1024 | bytes 1024 | tf_op jit(solution)/shard_map/weight_grad/pallas_call | solution.py:211
  588.2 14.3 %input_part.3 = (bf16[4,256,1024]{2,1,0:T(8,128)(2,1)}, bf16[4,256,1024]{2,1,0:T(8,128)(2,1)}) custom-call(s32[1]{0:T(128)} %bitcast.first, bf16[2048,2048]{1,0:T(8,128)(2,1)} %bitcast.113, bf16[2048,2048]{1,0:T(8,128)(2,1)} %bitcast.114, bf16[2048,1024]{1,0:T(8,128)(2,1)} %bitcast.129, f32[4,256,1024]{2,1,0:T(8,128)} %get-tuple-element.20.refs_0_, ...), custom_call_target="tpu_custom_call" | custom-call | flops 1024 | bytes 1024 | tf_op jit(solution)/shard_map/input_part/pallas_call | solution.py:315
  602.6 4.4 collective-permute-done.8
  606.9 3.9 add_convert_fusion
  610.9 4.6 all-to-all-start.6
  615.5 57.6 %reduce-scatter.10.cloned.1.call-done = bf16[1,256,1024]{2,1,0:T(8,128)(2,1)} async-done(((bf16[4,256,1024]{2,1,0:T(8,128)(2,1)}), bf16[1,256,1024]{2,1,0:T(8,128)(2,1)}) %reduce-scatter.10.cloned.1.call-update) | async-done | bytes 524304
  673.0 2.0 copy.102
  675.1 10.1 %all-to-all-done.6 = bf16[8,70,32,128]{3,2,1,0:T(8,128)(2,1)} async-done(((bf16[8,70,32,128]{3,2,1,0:T(8,128)(2,1)}), bf16[8,70,32,128]{3,2,1,0:T(8,128)(2,1)}, u32[]{:S(2)}, u32[]{:S(2)}) %all-to-all-start.6) | async-done | bytes 4587552 | tf_op jit(solution)/shard_map/all_to_all | solution.py:502
  685.2 3.5 all-to-all-start.5
  688.6 5.4 unpack.4.refs_0_
  694.1 5.4 unpack.5
  699.5 1.0 all-to-all-done.5
  700.8 1.0 copy.105
  (91 shorter events, 12.4 us)
Async XLA Ops:
  7.2 44.7 %copy-start.6 = (s32[3,128,26]{1,2,0:T(8,128)S(1)}, s32[3,128,26]{1,2,0:T(8,128)}, u32[]{:S(2)}) copy-start(s32[3,128,26]{1,2,0:T(8,128)} %param.13) | copy-start | bytes 119812
  7.2 45.0 %copy-start.2 = (s32[3,128,26]{1,2,0:T(8,128)S(1)}, s32[3,128,26]{1,2,0:T(8,128)}, u32[]{:S(2)}) copy-start(s32[3,128,26]{1,2,0:T(8,128)} %param.12) | copy-start | bytes 119812
  7.2 40.7 %all-gather.14.cloned.1.call-start = ((), (), s32[]{:S(2)}) async-start(), calls=%async_computation.15 | async-start | bytes 2621440 | tf_op jit(solution)/shard_map/all_gather | solution.py:465
  7.9 149.5 %all-gather.8.cloned.1.call-start = ((), (), s32[]{:S(2)}) async-start(), calls=%async_computation.10 | async-start | bytes 4718592 | tf_op jit(solution)/shard_map/all_gather | solution.py:474
  9.2 51.5 %copy-start.8 = (f32[3,416]{1,0:T(4,128)S(1)}, f32[3,416]{1,0:T(4,128)}, u32[]{:S(2)}) copy-start(f32[3,416]{1,0:T(4,128)} %param.10) | copy-start | bytes 14980
  9.6 39.6 %collective-permute-start = (bf16[256,256]{1,0:T(8,128)(2,1)S(1)}, bf16[256,256]{1,0:T(8,128)(2,1)S(1)}, u32[]{:S(2)}, u32[]{:S(2)}) collective-permute-start(bf16[256,256]{1,0:T(8,128)(2,1)S(1)} %bitcast.139), channel_id=1, source_target_pairs={{0,8},{8,16},{16,24},{24,0},{1,9},{9,17},{17,25},{25,1},{2,10},{10... | collective-permute-start | bytes 393224 | tf_op jit(solution)/shard_map/ppermute | solution.py:447
  12.8 36.4 %collective-permute-start.1 = (bf16[256,256]{1,0:T(8,128)(2,1)S(1)}, bf16[256,256]{1,0:T(8,128)(2,1)S(1)}, u32[]{:S(2)}, u32[]{:S(2)}) collective-permute-start(bf16[256,256]{1,0:T(8,128)(2,1)S(1)} %bitcast.140), channel_id=1, source_target_pairs={{0,16},{8,24},{16,0},{24,8},{1,17},{9,25},{17,1},{25,9},{2,18},{10... | collective-permute-start | bytes 393224 | tf_op jit(solution)/shard_map/ppermute | solution.py:447
  15.5 33.6 %collective-permute-start.2 = (bf16[256,256]{1,0:T(8,128)(2,1)S(1)}, bf16[256,256]{1,0:T(8,128)(2,1)S(1)}, u32[]{:S(2)}, u32[]{:S(2)}) collective-permute-start(bf16[256,256]{1,0:T(8,128)(2,1)S(1)} %bitcast.141), channel_id=1, source_target_pairs={{0,24},{8,0},{16,8},{24,16},{1,25},{9,1},{17,9},{25,17},{2,26},{10... | collective-permute-start | bytes 393224 | tf_op jit(solution)/shard_map/ppermute | solution.py:447
  49.2 0.6 copy-start.3
  49.2 0.7 copy-start.4
  49.2 0.7 copy-start.5
  67.5 4.8 copy-start.1
  67.5 69.3 %all-to-all-start = ((bf16[8,70,32,128]{3,2,1,0:T(8,128)(2,1)}), bf16[8,70,32,128]{3,2,1,0:T(8,128)(2,1)}, u32[]{:S(2)}, u32[]{:S(2)}) async-start(bf16[8,70,32,128]{3,2,1,0:T(8,128)(2,1)} %bitcast.115), calls=%async_computation | async-start | bytes 9175040 | tf_op jit(solution)/shard_map/all_to_all | solution.py:457
  72.3 205.2 %all-gather.16.cloned.1.call-start = ((), (), s32[]{:S(2)}) async-start(), calls=%async_computation.16 | async-start | bytes 7864320 | tf_op jit(solution)/shard_map/all_gather | solution.py:479
  72.4 16.6 %collective-permute-start.3 = (bf16[256,1024]{1,0:T(8,128)(2,1)S(1)}, bf16[256,1024]{1,0:T(8,128)(2,1)S(1)}, u32[]{:S(2)}, u32[]{:S(2)}) collective-permute-start(bf16[256,1024]{1,0:T(8,128)(2,1)S(1)} %copy-done.1), channel_id=1, source_target_pairs={{0,8},{8,16},{16,24},{24,0},{1,9},{9,17},{17,25},{25,1},{2,10},{10... | collective-permute-start | bytes 1572872 | tf_op jit(solution)/shard_map/ppermute | solution.py:447
  73.9 25.1 %collective-permute-start.5 = (bf16[256,1024]{1,0:T(8,128)(2,1)S(1)}, bf16[256,1024]{1,0:T(8,128)(2,1)S(1)}, u32[]{:S(2)}, u32[]{:S(2)}) collective-permute-start(bf16[256,1024]{1,0:T(8,128)(2,1)S(1)} %copy-done.1), channel_id=1, source_target_pairs={{0,24},{8,0},{16,8},{24,16},{1,25},{9,1},{17,9},{25,17},{2,26},{10... | collective-permute-start | bytes 1572872 | tf_op jit(solution)/shard_map/ppermute | solution.py:447
  76.2 45.8 %collective-permute-start.4 = (bf16[256,1024]{1,0:T(8,128)(2,1)S(1)}, bf16[256,1024]{1,0:T(8,128)(2,1)S(1)}, u32[]{:S(2)}, u32[]{:S(2)}) collective-permute-start(bf16[256,1024]{1,0:T(8,128)(2,1)S(1)} %copy-done.1), channel_id=1, source_target_pairs={{0,16},{8,24},{16,0},{24,8},{1,17},{9,25},{17,1},{25,9},{2,18},{10... | collective-permute-start | bytes 1572872 | tf_op jit(solution)/shard_map/ppermute | solution.py:447
  122.1 16.1 %copy-start.7 = (s32[3,128,26]{1,2,0:T(8,128)S(1)}, s32[3,128,26]{1,2,0:T(8,128)}, u32[]{:S(2)}) copy-start(s32[3,128,26]{1,2,0:T(8,128)} %param.11) | copy-start | bytes 119812
  138.2 221.2 %reduce-scatter.8.cloned.1.call-start = ((), (), s32[]{:S(2)}) async-start(), calls=%async_computation.12 | async-start | bytes 5242880 | tf_op jit(solution)/shard_map/reduce_scatter | solution.py:485
  180.8 221.2 %reduce-scatter.6.cloned.1.call-start = ((), (), s32[]{:S(2)}) async-start(), calls=%async_computation.11 | async-start | bytes 5242880 | tf_op jit(solution)/shard_map/reduce_scatter | solution.py:488
  277.5 58.1 %collective-permute-start.7 = (bf16[4,3,256,1024]{3,2,1,0:T(8,128)(2,1)}, bf16[4,3,256,1024]{3,2,1,0:T(8,128)(2,1)}, u32[]{:S(2)}, u32[]{:S(2)}) collective-permute-start(bf16[4,3,256,1024]{3,2,1,0:T(8,128)(2,1)} %tie.6.far), channel_id=1, source_target_pairs={{0,1},{1,0},{2,3},{3,2},{4,5},{5,4},{6,7},{7,6},{8,9},{9,8},{10,11... | collective-permute-start | bytes 18874376 | tf_op jit(solution)/shard_map/ppermute | solution.py:490
  277.5 5.0 copy-start
  277.5 58.1 %all-to-all-start.2 = ((bf16[8,70,32,128]{3,2,1,0:T(8,128)(2,1)}), bf16[8,70,32,128]{3,2,1,0:T(8,128)(2,1)}, u32[]{:S(2)}, u32[]{:S(2)}) async-start(bf16[8,70,32,128]{3,2,1,0:T(8,128)(2,1)} %tie.7), calls=%async_computation.2 | async-start | bytes 9175040 | tf_op jit(solution)/shard_map/all_to_all | solution.py:457
  282.3 206.7 %all-gather.12.cloned.1.call-start = ((), (), s32[]{:S(2)}) async-start(), calls=%async_computation.14 | async-start | bytes 5242880 | tf_op jit(solution)/shard_map/all_gather | solution.py:508
  282.5 9.1 %collective-permute-start.6 = (bf16[4,256,1024]{2,1,0:T(8,128)(2,1)S(1)}, bf16[4,256,1024]{2,1,0:T(8,128)(2,1)}, u32[]{:S(2)}, u32[]{:S(2)}) collective-permute-start(bf16[4,256,1024]{2,1,0:T(8,128)(2,1)S(1)} %bitcast.123), channel_id=1, source_target_pairs={{0,1},{1,0},{2,3},{3,2},{4,5},{5,4},{6,7},{7,6},{8,9},{9,8},{10,11... | collective-permute-start | bytes 6291464 | tf_op jit(solution)/shard_map/ppermute | solution.py:490
  428.2 58.0 %all-to-all-start.3 = ((bf16[8,70,32,128]{3,2,1,0:T(8,128)(2,1)}), bf16[8,70,32,128]{3,2,1,0:T(8,128)(2,1)}, u32[]{:S(2)}, u32[]{:S(2)}) async-start(bf16[8,70,32,128]{3,2,1,0:T(8,128)(2,1)} %bitcast.116), calls=%async_computation.5 | async-start | bytes 9175040 | tf_op jit(solution)/shard_map/all_to_all | solution.py:502
  432.9 137.0 %all-gather.10.cloned.1.call-start = ((), (), s32[]{:S(2)}) async-start(), calls=%async_computation.13 | async-start | bytes 5242880 | tf_op jit(solution)/shard_map/all_gather | solution.py:512
  507.2 57.9 %all-to-all-start.4 = ((bf16[8,70,32,128]{3,2,1,0:T(8,128)(2,1)}), bf16[8,70,32,128]{3,2,1,0:T(8,128)(2,1)}, u32[]{:S(2)}, u32[]{:S(2)}) async-start(bf16[8,70,32,128]{3,2,1,0:T(8,128)(2,1)} %bitcast.125), calls=%async_computation.6 | async-start | bytes 9175040 | tf_op jit(solution)/shard_map/all_to_all | solution.py:502
  511.8 161.2 %reduce-scatter.10.cloned.1.call-start = ((), (), s32[]{:S(2)}) async-start(), calls=%async_computation.17 | async-start | bytes 2621440
  602.6 4.4 collective-permute-start.8
  610.9 74.3 %all-to-all-start.6 = ((bf16[8,70,32,128]{3,2,1,0:T(8,128)(2,1)}), bf16[8,70,32,128]{3,2,1,0:T(8,128)(2,1)}, u32[]{:S(2)}, u32[]{:S(2)}) async-start(bf16[8,70,32,128]{3,2,1,0:T(8,128)(2,1)} %bitcast.124), calls=%async_computation.8 | async-start | bytes 9175040 | tf_op jit(solution)/shard_map/all_to_all | solution.py:502
  685.2 15.4 %all-to-all-start.5 = ((bf16[4,256,256]{1,2,0:T(8,128)(2,1)}), bf16[4,256,256]{1,2,0:T(8,128)(2,1)S(1)}, u32[]{:S(2)}, u32[]{:S(2)}) async-start(bf16[4,256,256]{1,2,0:T(8,128)(2,1)} %bitcast.64), calls=%async_computation.7 | async-start | bytes 1048576 | tf_op jit(solution)/shard_map/all_to_all | solution.py:541
Sparse Core Ops, SparseCore 0:
  9.9 38.0 all-gather.13
  52.0 47.8 all-gather.7
  138.3 102.9 all-gather.15
  243.5 79.0 reduce-scatter.7
  324.8 77.2 reduce-scatter.5
  407.7 81.2 all-gather.11
  490.5 79.2 all-gather.9
  611.0 62.0 reduce-scatter.9
where the time goes:
time: 711 us; the launch traced here: 709 us
  waiting for transfers between devices  339 us (48%)
  Pallas kernels  184 us (26%)
  blocking collectives  75.3 us (11%)
  starting transfers between devices  39.6 us (6%)
  local copies, waits for them, and re-layouts  36.1 us (5%)
  other arithmetic  19.8 us (3%)
  between operations  14.5 us (2%)
    all_to_all x3, waiting for transfers between devices, give_back(): lax.all_to_all(leaving, 'own', split_axis=0, concat_axis=0, tiled=True)  85.7 us
    all_to_all x1, blocking collectives, receive(): lax.all_to_all(sending, 'own', split_axis=0, concat_axis=0, tiled=True)  75.3 us
    unnamed x9, waiting for transfers between devices  59.1 us
    all_to_all x2, waiting for transfers between devices, receive(): lax.all_to_all(sending, 'own', split_axis=0, concat_axis=0, tiled=True)  57.5 us
    ppermute x6, waiting for transfers between devices, exchange(): kept.append(lax.ppermute(parts[s], 'dp', turn))  45.2 us
    reduce_scatter x1, waiting for transfers between devices, per_device(): up_value = lax.psum_scatter(part, 'dp', scatter_dimension=0)  42.7 us
    pallas_call x2, Pallas kernels, forward(): pl.pallas_call(kernel, out_shape=(jax.ShapeDtypeStruct((row_blocks, rows_...  37.5 us
    pallas_call x2, Pallas kernels, weight_grad(): pl.pallas_call(kernel, out_shape=(jax.ShapeDtypeStruct((places, rows_each...  36.6 us
  transfers between devices with their start and end apart: 23, of which 16 were waited for; matrix products, arithmetic and copies ran while one was open for 6% of the time, Pallas kernels for 21%

commit v1 on v0

--- a/solution.py
+++ b/solution.py
@@ -124,7 +124,7 @@
     )(flat, rows, x, arrived, *after)
 
 
-def forward_down(cotangents, arrived, flat, rows, quarter, first, columns, row_blocks):
+def forward_down(cotangents, arrived, flat, rows, quarter, order, columns, row_blocks):
     (near, far), _ = cotangents
     chips, tokens, width = near.shape
     planes = far.shape[1] + 1
@@ -134,7 +134,7 @@
     hidden = columns * rows_each
     per_owner = row_blocks // owners
 
-    def kernel(flat, rows, quarter, first, near, far, near_other, far_other, arrived, out, dense):
+    def kernel(flat, rows, quarter, order, near, far, near_other, far_other, arrived, out, dense):
         step = pl.program_id(0)
 
         @pl.when(step == 0)
@@ -154,7 +154,7 @@
                 lax.fori_loop(0, keep, place, 0, unroll=2)
 
         for core, (own, others) in enumerate(((near, far), (near_other, far_other))):
-            weights = dense[2 * step + lax.rem(first[0] + core, 2)]
+            weights = dense[order[2 * step + core]]
             for shift in range(planes):
                 cotangent = own[0] if shift == 0 else others[0, shift - 1]
                 plane = lax.rem(quarter[0] + planes - shift, planes)
@@ -164,7 +164,7 @@
                 )
 
     share = [
-        pl.BlockSpec((1, tokens, width), lambda g, *_: (g, 0, 0)),
+        pl.BlockSpec((1, tokens, width), lambda g, f, r, q, o: (o[2 * g] // 2, 0, 0)),
         pl.BlockSpec((1, planes - 1, tokens, width), lambda g, *_: (g, 0, 0, 0)),
     ]
     return pl.pallas_call(
@@ -180,7 +180,7 @@
         compiler_params=PARAMS,
         cost_estimate=COST,
         name="forward_down",
-    )(flat, rows, quarter, first, *cotangents[0], *cotangents[1], arrived)
+    )(flat, rows, quarter, order, *cotangents[0], *cotangents[1], arrived)
 
 
 def weight_grad(x_turned, grad, flat, rows, places, row_blocks, factor, after=()):
@@ -190,12 +190,11 @@
     keep = flat.shape[0] // columns
 
     def kernel(flat, rows, x_turned, grad, *refs):
-        out, natural, result = refs[-3:]
+        out, result = refs[-2:]
         step = pl.program_id(0)
-        for half in range(2):
-            for q in range(quarters):
-                natural[half, q] = grad[q, half]
-        right = natural[...].reshape(2 * block, tokens)
+        right = jnp.concatenate(
+            [grad[q, half] for half in range(2) for q in range(quarters)], axis=0
+        )
         product = lax.dot_general(x_turned[...], right, NT, preferred_element_type=F32)
         result[...] = (product * factor).astype(BF16).reshape(result.shape)
         for half in range(2):
@@ -210,10 +209,7 @@
 
     return pl.pallas_call(
         kernel,
-        out_shape=(
-            jax.ShapeDtypeStruct((places, rows_each, block), BF16),
-            jax.ShapeDtypeStruct((columns, quarters, rows_each, tokens), BF16),
-        ),
+        out_shape=jax.ShapeDtypeStruct((places, rows_each, block), BF16),
         grid_spec=pltpu.PrefetchScalarGridSpec(
             num_scalar_prefetch=2,
             grid=(columns // 2,),
@@ -222,10 +218,7 @@
                 pl.BlockSpec((quarters, 2, rows_each, tokens), lambda g, f, r: (0, g, 0, 0)),
             ]
             + waiting(after),
-            out_specs=(
-                whole((places, rows_each, block)),
-                pl.BlockSpec((2, quarters, rows_each, tokens), lambda g, f, r: (g, 0, 0, 0)),
-            ),
+            out_specs=whole((places, rows_each, block)),
             scratch_shapes=[pltpu.VMEM((row_blocks, rows_each, 2 * block), BF16)],
         ),
         compiler_params=PARAMS,
@@ -235,7 +228,7 @@
 
 
 def weight_grad_down(
-    value, cotangents, flat, rows, quarter, first, places, block, columns, row_blocks, factor
+    value, cotangents, flat, rows, quarter, order, places, block, columns, row_blocks, factor
 ):
     (near, far), _ = cotangents
     chips, tokens, width = near.shape
@@ -247,7 +240,7 @@
     per_owner = row_blocks // owners
 
     def kernel(
-        flat, rows, quarter, first, value, near, far, near_other, far_other, out, joined, result
+        flat, rows, quarter, order, value, near, far, near_other, far_other, out, joined, result
     ):
         step = pl.program_id(0)
         for core, (own, others) in enumerate(((near, far), (near_other, far_other))):
@@ -256,7 +249,7 @@
                 joined[lax.rem(quarter[0] + planes - shift, planes)] = cotangent
             right = joined[...].reshape(planes * tokens, width)
             product = jnp.dot(value[...], right, preferred_element_type=F32)
-            result[2 * step + lax.rem(first[0] + core, 2)] = (product * factor).astype(BF16)
+            result[order[2 * step + core]] = (product * factor).astype(BF16)
 
         @pl.when(step == chips - 1)
         def _():
@@ -273,7 +266,7 @@
                 lax.fori_loop(0, keep, place, 0, unroll=2)
 
     share = [
-        pl.BlockSpec((1, tokens, width), lambda g, *_: (g, 0, 0)),
+        pl.BlockSpec((1, tokens, width), lambda g, f, r, q, o: (o[2 * g] // 2, 0, 0)),
         pl.BlockSpec((1, planes - 1, tokens, width), lambda g, *_: (g, 0, 0, 0)),
     ]
     return pl.pallas_call(
@@ -292,18 +285,27 @@
         compiler_params=PARAMS,
         cost_estimate=COST,
         name="weight_grad_down",
-    )(flat, rows, quarter, first, value, *cotangents[0], *cotangents[1])
-
-
-def input_part(weights, grad, first, chips, earlier=()):
+    )(flat, rows, quarter, order, value, *cotangents[0], *cotangents[1])
+
+
+def input_part(weights, grad, first, chips, earlier=(), after=()):
     depth, units = weights.shape
-    tokens = grad.shape[1]
+    quarters, columns, rows_each, tokens = grad.shape
     rows = depth // (2 * chips)
 
     def kernel(first, left, right, grad, *refs):
-        earlier, outs = refs[:-2], refs[-2:]
+        earlier, (*outs, natural) = refs[: len(refs) - len(after) - 3], refs[-3:]
+
+        @pl.when(pl.program_id(0) == 0)
+        def _():
+            for c in range(columns):
+                for q in range(quarters):
+                    natural[c, q] = grad[q, c]
+
         both = jnp.concatenate([left[...], right[...]], axis=0)
-        product = jnp.dot(both, grad[...], preferred_element_type=F32)
+        product = jnp.dot(
+            both, natural[...].reshape(units, tokens), preferred_element_type=F32
+        )
         for core in range(2):
             part = product[core * rows : (core + 1) * rows]
             if earlier:
@@ -321,15 +323,17 @@
             in_specs=[
                 pl.BlockSpec((rows, units), lambda g, f: (2 * g + f[0], 0)),
                 pl.BlockSpec((rows, units), lambda g, f: (2 * g + 1 - f[0], 0)),
-                whole((units, tokens)),
+                whole(grad.shape),
             ]
-            + [share] * len(earlier),
+            + [share] * len(earlier)
+            + waiting(after),
             out_specs=(share, share),
+            scratch_shapes=[pltpu.VMEM((columns, quarters, rows_each, tokens), BF16)],
         ),
         compiler_params=PARAMS,
         cost_estimate=COST,
         name="input_part",
-    )(first, weights, weights, grad, *earlier)
+    )(first, weights, weights, grad, *earlier, *after)
 
 
 def unpack(which, returned, source, total):
@@ -461,8 +465,11 @@
     likes = [[core + 2 * chip for chip in range(chips)] for core in range(2)]
     swap = [(i, i ^ 1) for i in range(own_count)]
     core = jnp.remainder(own_index, 2).astype(jnp.int32).reshape(1)
+    turns = own_index ^ (2 * jnp.arange(chips, dtype=jnp.int32))
+    order = jnp.stack([turns, turns ^ 1], axis=1).reshape(own_count)
 
     near = lax.all_gather(out_grad, "own", axis=0, axis_index_groups=likes)
+    far = jnp.stack(exchange([out_grad] * data_count)[1:])
 
     local = inputs.reshape(local_tokens, row_blocks // own_count, data_count, rows_each)
     local = local.transpose(2, 0, 1, 3).reshape(data_count, local_tokens, depth // own_count)
@@ -470,27 +477,31 @@
     local = exchange(
         [lax.dynamic_index_in_dim(twice, data_index + s, 0, keepdims=False) for s in range(data_count)]
     )
-    local = in_order(local, quarter, (mark(near),))
+    sending_gate = send(0)
+    local = in_order(local, quarter, (mark(sending_gate), mark(far)))
     gathered = lax.all_gather(local.reshape(tokens, depth // own_count), "own", axis=0)
-    sending_gate, sending_up, sending_down = send(0), send(1, (mark(local),)), send(2, (mark(local),))
+    sending_up, sending_down = send(1, (mark(local),)), send(2, (mark(local),))
     arrived_gate = receive(sending_gate)
 
-    far = tie(jnp.stack(exchange([out_grad] * data_count)[1:]), mark(arrived_gate))
-    far = lax.all_gather(far, "own", axis=0, axis_index_groups=likes)
+    far = [tie(far, mark(arrived_gate))]
+    for turn in range(1, chips):
+        far.append(lax.ppermute(far[0], "own", [(i, i ^ (2 * turn)) for i in range(own_count)]))
 
     x = gathered.transpose(1, 0, 2).reshape(tokens, depth)
     x_turned = gathered.transpose(0, 2, 1).reshape(depth, tokens)
-    packed = (mark(sending_up), mark(sending_down))
+    packed = (mark(sending_up), mark(sending_down), mark(near))
     gate_weights, part = forward(x, arrived_gate, flat[0], rows[0], columns, row_blocks, packed)
     gate = lax.psum_scatter(part, "dp", scatter_dimension=0)
     arrived_up = receive(tie(sending_up, mark(gate_weights)))
-    up_weights, part = forward(x, arrived_up, flat[1], rows[1], columns, row_blocks)
+    up_weights, part = forward(
+        x, arrived_up, flat[1], rows[1], columns, row_blocks, (mark(gate),)
+    )
     up_value = lax.psum_scatter(part, "dp", scatter_dimension=0)
-    far = tie(far, mark(up_weights))
+    far = jnp.stack([tie(part, mark(up_weights)) for part in far])
     cotangents = ((near, far), (lax.ppermute(near, "own", swap), lax.ppermute(far, "own", swap)))
-    arrived_down = receive(tie(sending_down, mark(up_weights)))
+    arrived_down = receive(tie(sending_down, mark(arrived_up)))
     grad_act = forward_down(
-        cotangents, arrived_down, flat[2], rows[2], quarter, core, columns, row_blocks
+        cotangents, arrived_down, flat[2], rows[2], quarter, order, columns, row_blocks
     )
     value, grad_gate, grad_up = silu_parts(
         gate.reshape(hidden, tokens).astype(F32), up_value.reshape(hidden, tokens).astype(F32), grad_act
@@ -502,42 +513,34 @@
         returned = lax.all_to_all(leaving, "own", split_axis=0, concat_axis=0, tiled=True)
         return returned.reshape(places, rows_each, block)
 
-    def natural(grad):
-        return grad.reshape(columns * block, tokens)
-
     all_up = lax.all_gather(grad_up.reshape(shape), "dp", axis=0)
     leaving = weight_grad_down(
-        value, cotangents, flat[2], rows[2], quarter, core, places, block, columns, row_blocks, factor
+        value, cotangents, flat[2], rows[2], quarter, order, places, block, columns, row_blocks, factor
     )
     all_gate = lax.all_gather(grad_gate.reshape(shape), "dp", axis=0)
     returned = give_back(leaving)
-    leaving, whole_up = weight_grad(
+    leaving = weight_grad(
         x_turned, all_up, flat[1], rows[1], places, row_blocks, factor, (mark(returned),)
     )
     total = unpack(2, returned, source[2], None)
     returned = give_back(leaving)
+
     up_weights = up_weights.reshape(depth, columns * block)
-    back = input_part(up_weights, natural(whole_up), core, chips)
-    leaving, whole_gate = weight_grad(
-        x_turned,
-        all_gate,
-        flat[0],
-        rows[0],
-        places,
-        row_blocks,
-        factor,
-        (mark(returned), mark(back[0]), mark(total)),
+    gate_weights = gate_weights.reshape(depth, columns * block)
+    back = input_part(up_weights, all_up, core, chips, after=(mark(leaving),))
+    back = input_part(gate_weights, all_gate, core, chips, back, (mark(returned), mark(total)))
+    leaving = weight_grad(
+        x_turned, all_gate, flat[0], rows[0], places, row_blocks, factor, (mark(back[0]),)
     )
     total = unpack(1, returned, source[1], total)
     returned = give_back(leaving)
 
-    gate_weights = gate_weights.reshape(depth, columns * block)
-    back = input_part(gate_weights, natural(whole_gate), core, chips, back)
     back = back[0].astype(F32) + lax.ppermute(back[1], "own", swap).astype(F32)
     back = lax.psum_scatter(
         back.astype(BF16), "own", scatter_dimension=0, axis_index_groups=likes
     )
     back = back.reshape(depth // own_count, data_count, local_tokens).transpose(1, 0, 2)
+    back = tie(back, mark(total))
     back = lax.all_to_all(back, "dp", split_axis=0, concat_axis=0, tiled=True)
     back = back.reshape(data_count, row_blocks // own_count, rows_each, local_tokens)
     input_grad = back.transpose(3, 1, 0, 2).reshape(local_tokens, local_width)

time: 711 us -> 700 us (0.985)
  blocking collectives: 75.3 us -> 0 us
  waiting for transfers between devices: 339 us -> 379 us
  local copies, waits for them, and re-layouts: 36.1 us -> 46.9 us
  starting transfers between devices: 39.6 us -> 48.3 us
    all_to_all x1 -> x0, blocking collectives: 75.3 us -> none  [receive(): lax.all_to_all(sending, 'own', split_axis=0, concat_axis=0, tiled=True)]
    all_gather x1, waiting for transfers between devices: 0.01 us -> 52.5 us  [per_device(): lax.all_gather(local.reshape(tokens, depth // own_count), 'own', axis=0)]
    unnamed x9 -> x8, waiting for transfers between devices: 59.1 us -> 10.2 us
    ppermute x0 -> x3, waiting for transfers between devices: none -> 45.6 us  [per_device(): lax.ppermute(far[0], 'own', [(i, i ^ 2 * turn) for i in range(own_count)])]
    ppermute x6, waiting for transfers between devices: 45.2 us -> 90.3 us  [exchange(): kept.append(lax.ppermute(parts[s], 'dp', turn))]
    reduce_scatter x1, waiting for transfers between devices: 42.7 us -> 0.01 us  [per_device(): up_value = lax.psum_scatter(part, 'dp', scatter_dimension=0)]
    all_to_all x3, waiting for transfers between devices: 85.7 us -> 117 us  [give_back(): lax.all_to_all(leaving, 'own', split_axis=0, concat_axis=0, tiled=True)]
    all_gather x1, waiting for transfers between devices: 30.2 us -> 0.01 us  [per_device(): near = lax.all_gather(out_grad, 'own', axis=0, axis_index_groups=likes)]
  transfers between devices with their start and end apart: 23 -> 26, of which waited for: 16 -> 16; matrix products, arithmetic and copies ran while one was open for 6% -> 8% of each run, Pallas kernels for 21% -> 22%
where the time goes in v1:
time: 700 us; the launch traced here: 697 us
  waiting for transfers between devices  379 us (54%)
  Pallas kernels  184 us (26%)
  starting transfers between devices  48.3 us (7%)
  local copies, waits for them, and re-layouts  46.9 us (7%)
  other arithmetic  23.8 us (3%)
  between operations  14.5 us (2%)
    all_to_all x3, waiting for transfers between devices, give_back(): lax.all_to_all(leaving, 'own', split_axis=0, concat_axis=0, tiled=True)  117 us
    ppermute x6, waiting for transfers between devices, exchange(): kept.append(lax.ppermute(parts[s], 'dp', turn))  90.3 us
    all_gather x1, waiting for transfers between devices, per_device(): lax.all_gather(local.reshape(tokens, depth // own_count), 'own', axis=0)  52.5 us
    ppermute x3, waiting for transfers between devices, per_device(): lax.ppermute(far[0], 'own', [(i, i ^ 2 * turn) for i in range(own_count)])  45.6 us
    all_to_all x3, waiting for transfers between devices, receive(): lax.all_to_all(sending, 'own', split_axis=0, concat_axis=0, tiled=True)  45.3 us
    pallas_call x2, Pallas kernels, forward(): pl.pallas_call(kernel, out_shape=(jax.ShapeDtypeStruct((row_blocks, rows_...  37.4 us
    pallas_call x2, Pallas kernels, weight_grad(): pl.pallas_call(kernel, out_shape=jax.ShapeDtypeStruct((places, rows_each,...  36 us
    pallas_call x2, Pallas kernels, input_part(): pl.pallas_call(kernel, out_shape=(out, out), grid_spec=pltpu.PrefetchScal...  28.5 us
  transfers between devices with their start and end apart: 26, of which 16 were waited for; matrix products, arithmetic and copies ran while one was open for 8% of the time, Pallas kernels for 22%

profile of v1, /device:TPU:0, one launch (start us, length us, event | category | flops | bytes accessed | tf_op | source)
XLA Modules:
  0.0 696.9 jit_solution(11318453128708263233)
XLA Ops:
  8.0 3.1 collective-permute-start.3
  12.7 1.6 collective-permute-start
  15.6 3.0 collective-permute-start.2
  19.2 3.4 reduce-window.6
  23.1 3.6 select_reduce_fusion.1
  28.0 6.2 pack.3
  34.9 1.3 slice_bitcast_fusion.13.refs_4_
  37.6 1.9 in_order.1
  39.5 4.8 all-to-all-start
  47.9 1.3 slice_bitcast_fusion.11.refs_0_
  49.2 6.2 pack.5
  55.5 6.1 pack.4
  61.6 1.3 slice_bitcast_fusion.9
  62.9 1.3 slice_bitcast_fusion.8.refs_2_
  64.1 52.5 %all-gather.6.cloned.1.call-done = bf16[8,1024,256]{2,1,0:T(8,128)(2,1)} async-done(((bf16[1,1024,256]{2,1,0:T(8,128)(2,1)}), bf16[8,1024,256]{2,1,0:T(8,128)(2,1)}) %all-gather.6.cloned.1.call-update) | async-done | bytes 4194320 | tf_op jit(solution)/shard_map/all_gather | solution.py:482
  116.6 4.8 copy.87
  121.5 18.7 %forward.2 = (bf16[64,32,2048]{2,1,0:T(8,128)(2,1)}, bf16[4,16,32,1024]{3,2,1,0:T(8,128)(2,1)}) custom-call(s32[416]{0:T(512)} %bitcast.169, s32[416]{0:T(512)} %bitcast.165, bf16[1024,2048]{1,0:T(8,128)(2,1)} %bitcast.121, bf16[560,32,128]{2,1,0:T(8,128)(2,1)} %bitcast.20.arrived, bf16[16,128]{1,0:T(8,128)(2,1)} %get-tuple-element.53.refs_0_, ...), custom_call_target="tpu_custom_call" | custom-call | flops 1024 | bytes 1024 | tf_op jit(solution)/shard_map/forward/pallas_call | solution.py:106
  140.2 1.3 slice_bitcast_fusion.16.refs_1_
  141.4 4.7 all-to-all-start.1
  146.2 3.4 collective-permute-start.5
  149.6 30.6 %collective-permute-done.5 = bf16[256,1024]{1,0:T(8,128)(2,1)S(1)} collective-permute-done((bf16[256,1024]{1,0:T(8,128)(2,1)S(1)}, bf16[256,1024]{1,0:T(8,128)(2,1)S(1)}, u32[]{:S(2)}, u32[]{:S(2)}) %collective-permute-start.5) | collective-permute-done | bytes 524320 | tf_op jit(solution)/shard_map/ppermute | solution.py:451
  180.2 59.6 %collective-permute-done.4 = bf16[256,1024]{1,0:T(8,128)(2,1)S(1)} collective-permute-done((bf16[256,1024]{1,0:T(8,128)(2,1)S(1)}, bf16[256,1024]{1,0:T(8,128)(2,1)S(1)}, u32[]{:S(2)}, u32[]{:S(2)}) %collective-permute-start.4) | collective-permute-done | bytes 524320 | tf_op jit(solution)/shard_map/ppermute | solution.py:451
  239.8 1.3 pad_maximum_fusion.1.refs_0_
  241.2 1.3 slice_bitcast_fusion.7.refs_1_
  242.4 2.4 collective-permute-start.8
  247.0 1.3 slice_bitcast_fusion.6.refs_0_
  248.3 18.7 %forward.3 = (bf16[64,32,2048]{2,1,0:T(8,128)(2,1)}, bf16[4,16,32,1024]{3,2,1,0:T(8,128)(2,1)}) custom-call(s32[416]{0:T(512)} %bitcast.171, s32[416]{0:T(512)} %bitcast.167, bf16[1024,2048]{1,0:T(8,128)(2,1)} %bitcast.122, bf16[560,32,128]{2,1,0:T(8,128)(2,1)} %bitcast.38.arrived, bf16[16,128]{1,0:T(8,128)(2,1)} %slice_bitcast_fusion.6.refs_0_), custom_call_target="tpu_custom_call" | custom-call | flops 1024 | bytes 1024 | tf_op jit(solution)/shard_map/forward/pallas_call | solution.py:106
  267.0 1.3 slice_bitcast_fusion.15.refs_1_
  268.2 12.6 %collective-permute-done.8.refs_0_ = bf16[3,256,1024]{2,1,0:T(8,128)(2,1)S(1)} collective-permute-done((bf16[3,256,1024]{2,1,0:T(8,128)(2,1)}, bf16[3,256,1024]{2,1,0:T(8,128)(2,1)S(1)}, u32[]{:S(2)}, u32[]{:S(2)}) %collective-permute-start.8) | collective-permute-done | bytes 1572896 | tf_op jit(solution)/shard_map/ppermute | solution.py:488
  280.9 32.5 %collective-permute-done.7.refs_0_ = bf16[3,256,1024]{2,1,0:T(8,128)(2,1)S(1)} collective-permute-done((bf16[3,256,1024]{2,1,0:T(8,128)(2,1)}, bf16[3,256,1024]{2,1,0:T(8,128)(2,1)S(1)}, u32[]{:S(2)}, u32[]{:S(2)}) %collective-permute-start.7) | collective-permute-done | bytes 1572896 | tf_op jit(solution)/shard_map/ppermute | solution.py:488
  314.6 1.4 copy-done
  317.0 4.3 pad_maximum_fusion.far
  321.4 1.3 slice_bitcast_fusion.5.refs_1_
  322.7 4.7 all-to-all-start.2
  328.7 6.7 collective-permute-done.9.near_other
  335.4 45.3 %all-to-all-done.2 = bf16[8,70,32,128]{3,2,1,0:T(8,128)(2,1)} async-done(((bf16[8,70,32,128]{3,2,1,0:T(8,128)(2,1)}), bf16[8,70,32,128]{3,2,1,0:T(8,128)(2,1)}, u32[]{:S(2)}, u32[]{:S(2)}) %all-to-all-start.2) | async-done | bytes 4587552 | tf_op jit(solution)/shard_map/all_to_all | solution.py:461
  380.7 24.2 %forward_down.1 = f32[512,1024]{1,0:T(8,128)} custom-call(s32[416]{0:T(512)} %bitcast.163, s32[416]{0:T(512)} %bitcast.161, s32[1]{0:T(128)} %bitcast.3.quarter, s32[8]{0:T(128)} %reshape.181.order, bf16[4,256,1024]{2,1,0:T(8,128)(2,1)} %bitcast.137, bf16[4,3,256,1024]{3,2,1,0:T(8,128)(2,1)} %pad_maximum_fusion.far, ...), custom_call_target="tpu_custom_call" | custom-call | flops 1024 | bytes 1024 | tf_op jit(solution)/shard_map/forward_down/pallas_call | solution.py:170
  404.9 5.1 multiply_convert_fusion
  410.1 21.2 %weight_grad_down.1 = bf16[560,32,128]{2,1,0:T(8,128)(2,1)} custom-call(s32[416]{0:T(512)} %bitcast.164, s32[416]{0:T(512)} %bitcast.162, s32[1]{0:T(128)} %bitcast.3.quarter, s32[8]{0:T(128)} %reshape.181.order, bf16[512,1024]{1,0:T(8,128)(2,1)} %get-tuple-element.30.value, bf16[4,256,1024]{2,1,0:T(8,128)(2,1)} %bitcast.138, ...), custom_call_target="tpu_custom_call" | custom-call | flops 1024 | bytes 1024 | tf_op jit(solution)/shard_map/weight_grad_down/pallas_call | solution.py:272
  431.3 4.6 all-to-all-start.3
  436.5 6.5 copy.81
  442.9 46.3 %all-to-all-done.3 = bf16[8,70,32,128]{3,2,1,0:T(8,128)(2,1)} async-done(((bf16[8,70,32,128]{3,2,1,0:T(8,128)(2,1)}), bf16[8,70,32,128]{3,2,1,0:T(8,128)(2,1)}, u32[]{:S(2)}, u32[]{:S(2)}) %all-to-all-start.3) | async-done | bytes 4587552 | tf_op jit(solution)/shard_map/all_to_all | solution.py:513
  489.2 1.3 slice_bitcast_fusion.4.refs_0_
  490.5 18.0 %weight_grad.2 = bf16[560,32,128]{2,1,0:T(8,128)(2,1)} custom-call(s32[416]{0:T(512)} %bitcast.172, s32[416]{0:T(512)} %bitcast.168, bf16[2048,1024]{1,0:T(8,128)(2,1)} %bitcast.123, bf16[4,16,32,1024]{3,2,1,0:T(8,128)(2,1)} %all-gather.10.cloned.1.call-done.grad, bf16[16,128]{1,0:T(8,128)(2,1)} %slice_bitcast_fusion.4.refs_0_), custom_call_target="tpu_custom_call" | custom-call | flops 1024 | bytes 1024 | tf_op jit(solution)/shard_map/weight_grad/pallas_call | solution.py:210
  508.5 4.6 all-to-all-start.4
  515.3 5.4 unpack.3.refs_0_
  520.7 1.3 slice_bitcast_fusion.1.refs_3_
  522.0 1.3 slice_bitcast_fusion.3.refs_0_
  523.3 13.9 %input_part.2 = (f32[4,256,1024]{2,1,0:T(8,128)}, f32[4,256,1024]{2,1,0:T(8,128)}) custom-call(s32[1]{0:T(128)} %bitcast.first, bf16[2048,2048]{1,0:T(8,128)(2,1)} %bitcast.127, bf16[2048,2048]{1,0:T(8,128)(2,1)} %bitcast.128, bf16[4,16,32,1024]{3,2,1,0:T(8,128)(2,1)} %all-gather.10.cloned.1.call-done.grad, bf16[16,128]{1,0:T(8,128)(2,1)} %slice_bitcast_fusion.3.refs_0_), custom_call_target="tpu_custom_call" | custom-call | flops 1024 | bytes 1024 | tf_op jit(solution)/shard_map/input_part/pallas_call | solution.py:317
  537.2 29.2 %all-to-all-done.4 = bf16[8,70,32,128]{3,2,1,0:T(8,128)(2,1)} async-done(((bf16[8,70,32,128]{3,2,1,0:T(8,128)(2,1)}), bf16[8,70,32,128]{3,2,1,0:T(8,128)(2,1)}, u32[]{:S(2)}, u32[]{:S(2)}) %all-to-all-start.4) | async-done | bytes 4587552 | tf_op jit(solution)/shard_map/all_to_all | solution.py:513
  566.5 1.3 slice_bitcast_fusion.2.refs_2_
  568.1 14.6 %input_part.3 = (bf16[4,256,1024]{2,1,0:T(8,128)(2,1)}, bf16[4,256,1024]{2,1,0:T(8,128)(2,1)}) custom-call(s32[1]{0:T(128)} %bitcast.first, bf16[2048,2048]{1,0:T(8,128)(2,1)} %bitcast.125, bf16[2048,2048]{1,0:T(8,128)(2,1)} %bitcast.126, bf16[4,16,32,1024]{3,2,1,0:T(8,128)(2,1)} %all-gather.8.cloned.1.call-done.grad, ...), custom_call_target="tpu_custom_call" | custom-call | flops 1024 | bytes 1024 | tf_op jit(solution)/shard_map/input_part/pallas_call | solution.py:317
  582.7 4.4 collective-permute-done.11
  587.0 3.9 add_convert_fusion
  590.9 1.3 slice_bitcast_fusion.14.refs_0_
  592.2 17.9 %weight_grad.3 = bf16[560,32,128]{2,1,0:T(8,128)(2,1)} custom-call(s32[416]{0:T(512)} %bitcast.170, s32[416]{0:T(512)} %bitcast.166, bf16[2048,1024]{1,0:T(8,128)(2,1)} %bitcast.124, bf16[4,16,32,1024]{3,2,1,0:T(8,128)(2,1)} %all-gather.8.cloned.1.call-done.grad, bf16[16,128]{1,0:T(8,128)(2,1)} %slice_bitcast_fusion.14.refs_0_), custom_call_target="tpu_custom_call" | custom-call | flops 1024 | bytes 1024 | tf_op jit(solution)/shard_map/weight_grad/pallas_call | solution.py:210
  610.1 4.6 all-to-all-start.6
  614.7 5.6 unpack.4.refs_0_
  620.3 1.3 slice_bitcast_fusion.refs_1_
  621.6 8.9 %reduce-scatter.10.cloned.1.call-done = bf16[1,256,1024]{2,1,0:T(8,128)(2,1)} async-done(((bf16[4,256,1024]{2,1,0:T(8,128)(2,1)}), bf16[1,256,1024]{2,1,0:T(8,128)(2,1)}) %reduce-scatter.10.cloned.1.call-update) | async-done | bytes 524304
  632.7 41.0 %all-to-all-done.6 = bf16[8,70,32,128]{3,2,1,0:T(8,128)(2,1)} async-done(((bf16[8,70,32,128]{3,2,1,0:T(8,128)(2,1)}), bf16[8,70,32,128]{3,2,1,0:T(8,128)(2,1)}, u32[]{:S(2)}, u32[]{:S(2)}) %all-to-all-start.6) | async-done | bytes 4587552 | tf_op jit(solution)/shard_map/all_to_all | solution.py:513
  673.7 3.5 all-to-all-start.5
  677.1 5.4 unpack.5
  682.6 6.4 all-to-all-done.5
  (121 shorter events, 23.9 us)
Async XLA Ops:
  7.2 11.4 %copy-start.12 = (s32[3,128,26]{1,2,0:T(8,128)S(1)}, s32[3,128,26]{1,2,0:T(8,128)}, u32[]{:S(2)}) copy-start(s32[3,128,26]{1,2,0:T(8,128)} %param.13) | copy-start | bytes 119812
  7.2 11.7 %copy-start.8 = (s32[3,128,26]{1,2,0:T(8,128)S(1)}, s32[3,128,26]{1,2,0:T(8,128)}, u32[]{:S(2)}) copy-start(s32[3,128,26]{1,2,0:T(8,128)} %param.12) | copy-start | bytes 119812
  7.2 20.3 %copy-start.14 = (f32[3,416]{1,0:T(4,128)S(1)}, f32[3,416]{1,0:T(4,128)}, u32[]{:S(2)}) copy-start(f32[3,416]{1,0:T(4,128)} %param.10) | copy-start | bytes 14980
  7.2 55.7 %all-gather.12.cloned.1.call-start = ((), (), s32[]{:S(2)}) async-start(), calls=%async_computation.15 | async-start | bytes 2621440 | tf_op jit(solution)/shard_map/all_gather | solution.py:471
  7.9 108.7 %all-gather.6.cloned.1.call-start = ((), (), s32[]{:S(2)}) async-start(), calls=%async_computation.10 | async-start | bytes 4718592 | tf_op jit(solution)/shard_map/all_gather | solution.py:482
  8.0 28.3 %collective-permute-start.3 = (bf16[256,1024]{1,0:T(8,128)(2,1)}, bf16[256,1024]{1,0:T(8,128)(2,1)S(1)}, u32[]{:S(2)}, u32[]{:S(2)}) collective-permute-start(bf16[256,1024]{1,0:T(8,128)(2,1)} %param.8), channel_id=1, source_target_pairs={{0,8},{8,16},{16,24},{24,0},{1,9},{9,17},{17,25},{25,1},{2,10},{10... | collective-permute-start | bytes 1572872 | tf_op jit(solution)/shard_map/ppermute | solution.py:451
  12.7 24.1 %collective-permute-start = (bf16[256,256]{1,0:T(8,128)(2,1)S(1)}, bf16[256,256]{1,0:T(8,128)(2,1)S(1)}, u32[]{:S(2)}, u32[]{:S(2)}) collective-permute-start(bf16[256,256]{1,0:T(8,128)(2,1)S(1)} %bitcast.157), channel_id=1, source_target_pairs={{0,8},{8,16},{16,24},{24,0},{1,9},{9,17},{17,25},{25,1},{2,10},{10... | collective-permute-start | bytes 393224 | tf_op jit(solution)/shard_map/ppermute | solution.py:451
  14.4 22.4 %collective-permute-start.1 = (bf16[256,256]{1,0:T(8,128)(2,1)S(1)}, bf16[256,256]{1,0:T(8,128)(2,1)S(1)}, u32[]{:S(2)}, u32[]{:S(2)}) collective-permute-start(bf16[256,256]{1,0:T(8,128)(2,1)S(1)} %bitcast.158), channel_id=1, source_target_pairs={{0,16},{8,24},{16,0},{24,8},{1,17},{9,25},{17,1},{25,9},{2,18},{10... | collective-permute-start | bytes 393224 | tf_op jit(solution)/shard_map/ppermute | solution.py:451
  15.6 21.2 %collective-permute-start.2 = (bf16[256,256]{1,0:T(8,128)(2,1)S(1)}, bf16[256,256]{1,0:T(8,128)(2,1)S(1)}, u32[]{:S(2)}, u32[]{:S(2)}) collective-permute-start(bf16[256,256]{1,0:T(8,128)(2,1)S(1)} %bitcast.159), channel_id=1, source_target_pairs={{0,24},{8,0},{16,8},{24,16},{1,25},{9,1},{17,9},{25,17},{2,26},{10... | collective-permute-start | bytes 393224 | tf_op jit(solution)/shard_map/ppermute | solution.py:451
  36.8 0.6 copy-start.9
  36.8 0.7 copy-start.10
  36.8 0.7 copy-start.11
  39.5 4.8 copy-start.13
  39.5 81.9 %all-to-all-start = ((bf16[8,70,32,128]{3,2,1,0:T(8,128)(2,1)}), bf16[8,70,32,128]{3,2,1,0:T(8,128)(2,1)}, u32[]{:S(2)}, u32[]{:S(2)}) async-start(bf16[8,70,32,128]{3,2,1,0:T(8,128)(2,1)} %bitcast.130), calls=%async_computation | async-start | bytes 9175040 | tf_op jit(solution)/shard_map/all_to_all | solution.py:461
  44.3 202.7 %reduce-scatter.6.cloned.1.call-start = ((), (), s32[]{:S(2)}) async-start(), calls=%async_computation.11 | async-start | bytes 5242880 | tf_op jit(solution)/shard_map/reduce_scatter | solution.py:494
  141.4 4.8 copy-start.7
  141.4 106.8 %all-to-all-start.1 = ((bf16[8,70,32,128]{3,2,1,0:T(8,128)(2,1)}), bf16[8,70,32,128]{3,2,1,0:T(8,128)(2,1)}, u32[]{:S(2)}, u32[]{:S(2)}) async-start(bf16[8,70,32,128]{3,2,1,0:T(8,128)(2,1)} %tie.9), calls=%async_computation.1 | async-start | bytes 9175040 | tf_op jit(solution)/shard_map/all_to_all | solution.py:461
  146.1 258.8 %reduce-scatter.8.cloned.1.call-start = ((), (), s32[]{:S(2)}) async-start(), calls=%async_computation.12 | async-start | bytes 5242880 | tf_op jit(solution)/shard_map/reduce_scatter | solution.py:499
  146.2 34.0 %collective-permute-start.5 = (bf16[256,1024]{1,0:T(8,128)(2,1)S(1)}, bf16[256,1024]{1,0:T(8,128)(2,1)S(1)}, u32[]{:S(2)}, u32[]{:S(2)}) collective-permute-start(bf16[256,1024]{1,0:T(8,128)(2,1)S(1)} %copy-done.7), channel_id=1, source_target_pairs={{0,24},{8,0},{16,8},{24,16},{1,25},{9,1},{17,9},{25,17},{2,26},{10... | collective-permute-start | bytes 1572872 | tf_op jit(solution)/shard_map/ppermute | solution.py:451
  149.6 90.2 %collective-permute-start.4 = (bf16[256,1024]{1,0:T(8,128)(2,1)S(1)}, bf16[256,1024]{1,0:T(8,128)(2,1)S(1)}, u32[]{:S(2)}, u32[]{:S(2)}) collective-permute-start(bf16[256,1024]{1,0:T(8,128)(2,1)S(1)} %copy-done.7), channel_id=1, source_target_pairs={{0,16},{8,24},{16,0},{24,8},{1,17},{9,25},{17,1},{25,9},{2,18},{10... | collective-permute-start | bytes 1572872 | tf_op jit(solution)/shard_map/ppermute | solution.py:451
  242.4 38.4 %collective-permute-start.8 = (bf16[3,256,1024]{2,1,0:T(8,128)(2,1)}, bf16[3,256,1024]{2,1,0:T(8,128)(2,1)S(1)}, u32[]{:S(2)}, u32[]{:S(2)}) collective-permute-start(bf16[3,256,1024]{2,1,0:T(8,128)(2,1)} %tie.8.refs_0_), channel_id=1, source_target_pairs={{0,6},{1,7},{2,4},{3,5},{4,2},{5,3},{6,0},{7,1},{8,14},{9,15},{10,... | collective-permute-start | bytes 4718600 | tf_op jit(solution)/shard_map/ppermute | solution.py:488
  244.8 68.6 %collective-permute-start.7 = (bf16[3,256,1024]{2,1,0:T(8,128)(2,1)}, bf16[3,256,1024]{2,1,0:T(8,128)(2,1)S(1)}, u32[]{:S(2)}, u32[]{:S(2)}) collective-permute-start(bf16[3,256,1024]{2,1,0:T(8,128)(2,1)} %tie.8.refs_0_), channel_id=1, source_target_pairs={{0,4},{1,5},{2,6},{3,7},{4,0},{5,1},{6,2},{7,3},{8,12},{9,13},{10,... | collective-permute-start | bytes 4718600 | tf_op jit(solution)/shard_map/ppermute | solution.py:488
  245.4 68.5 %collective-permute-start.6 = (bf16[3,256,1024]{2,1,0:T(8,128)(2,1)}, bf16[3,256,1024]{2,1,0:T(8,128)(2,1)}, u32[]{:S(2)}, u32[]{:S(2)}) collective-permute-start(bf16[3,256,1024]{2,1,0:T(8,128)(2,1)} %tie.8.refs_0_), channel_id=1, source_target_pairs={{0,2},{1,3},{2,0},{3,1},{4,6},{5,7},{6,4},{7,5},{8,10},{9,11},{10,... | collective-permute-start | bytes 4718600 | tf_op jit(solution)/shard_map/ppermute | solution.py:488
  280.9 33.0 %copy-start.2 = (bf16[3,256,1024]{2,1,0:T(8,128)(2,1)}, bf16[3,256,1024]{2,1,0:T(8,128)(2,1)S(1)}, u32[]{:S(2)}) copy-start(bf16[3,256,1024]{2,1,0:T(8,128)(2,1)S(1)} %collective-permute-done.8.refs_0_) | copy-start | bytes 4718596
  313.4 1.2 copy-start.4
  314.6 1.4 copy-start
  314.6 1.9 copy-start.3
  314.6 2.4 copy-start.5
  321.3 59.4 %collective-permute-start.10 = (bf16[4,3,256,1024]{3,2,1,0:T(8,128)(2,1)}, bf16[4,3,256,1024]{3,2,1,0:T(8,128)(2,1)}, u32[]{:S(2)}, u32[]{:S(2)}) collective-permute-start(bf16[4,3,256,1024]{3,2,1,0:T(8,128)(2,1)} %pad_maximum_fusion.far), channel_id=1, source_target_pairs={{0,1},{1,0},{2,3},{3,2},{4,5},{5,4},{6,7},{7,6},{8,9},{9,8},{10,11... | collective-permute-start | bytes 18874376 | tf_op jit(solution)/shard_map/ppermute | solution.py:501
  322.7 4.9 copy-start.1
  322.7 58.0 %all-to-all-start.2 = ((bf16[8,70,32,128]{3,2,1,0:T(8,128)(2,1)}), bf16[8,70,32,128]{3,2,1,0:T(8,128)(2,1)}, u32[]{:S(2)}, u32[]{:S(2)}) async-start(bf16[8,70,32,128]{3,2,1,0:T(8,128)(2,1)} %tie.14), calls=%async_computation.3 | async-start | bytes 9175040 | tf_op jit(solution)/shard_map/all_to_all | solution.py:461
  327.4 163.1 %all-gather.10.cloned.1.call-start = ((), (), s32[]{:S(2)}) async-start(), calls=%async_computation.14 | async-start | bytes 5242880 | tf_op jit(solution)/shard_map/all_gather | solution.py:516
  327.6 7.8 %collective-permute-start.9 = (bf16[4,256,1024]{2,1,0:T(8,128)(2,1)S(1)}, bf16[4,256,1024]{2,1,0:T(8,128)(2,1)}, u32[]{:S(2)}, u32[]{:S(2)}) collective-permute-start(bf16[4,256,1024]{2,1,0:T(8,128)(2,1)S(1)} %bitcast.139), channel_id=1, source_target_pairs={{0,1},{1,0},{2,3},{3,2},{4,5},{5,4},{6,7},{7,6},{8,9},{9,8},{10,11... | collective-permute-start | bytes 6291464 | tf_op jit(solution)/shard_map/ppermute | solution.py:501
  380.7 24.2 %copy-start.6 = (bf16[1,16,32,1024]{3,2,1,0:T(8,128)(2,1)S(1)}, bf16[1,16,32,1024]{3,2,1,0:T(8,128)(2,1)}, u32[]{:S(2)}) copy-start(bf16[1,16,32,1024]{3,2,1,0:T(8,128)(2,1)} %reduce-scatter.6.cloned.1.call-done) | copy-start | bytes 3145732
  431.3 57.9 %all-to-all-start.3 = ((bf16[8,70,32,128]{3,2,1,0:T(8,128)(2,1)}), bf16[8,70,32,128]{3,2,1,0:T(8,128)(2,1)}, u32[]{:S(2)}, u32[]{:S(2)}) async-start(bf16[8,70,32,128]{3,2,1,0:T(8,128)(2,1)} %bitcast.132), calls=%async_computation.5 | async-start | bytes 9175040 | tf_op jit(solution)/shard_map/all_to_all | solution.py:513
  435.9 132.2 %all-gather.8.cloned.1.call-start = ((), (), s32[]{:S(2)}) async-start(), calls=%async_computation.13 | async-start | bytes 5242880 | tf_op jit(solution)/shard_map/all_gather | solution.py:520
  508.5 57.9 %all-to-all-start.4 = ((bf16[8,70,32,128]{3,2,1,0:T(8,128)(2,1)}), bf16[8,70,32,128]{3,2,1,0:T(8,128)(2,1)}, u32[]{:S(2)}, u32[]{:S(2)}) async-start(bf16[8,70,32,128]{3,2,1,0:T(8,128)(2,1)} %bitcast.131), calls=%async_computation.6 | async-start | bytes 9175040 | tf_op jit(solution)/shard_map/all_to_all | solution.py:513
  513.1 117.3 %reduce-scatter.10.cloned.1.call-start = ((), (), s32[]{:S(2)}) async-start(), calls=%async_computation.16 | async-start | bytes 2621440
  582.7 4.4 collective-permute-start.11
  610.1 63.6 %all-to-all-start.6 = ((bf16[8,70,32,128]{3,2,1,0:T(8,128)(2,1)}), bf16[8,70,32,128]{3,2,1,0:T(8,128)(2,1)}, u32[]{:S(2)}, u32[]{:S(2)}) async-start(bf16[8,70,32,128]{3,2,1,0:T(8,128)(2,1)} %bitcast.133), calls=%async_computation.8 | async-start | bytes 9175040 | tf_op jit(solution)/shard_map/all_to_all | solution.py:513
  673.7 15.3 %all-to-all-start.5 = ((bf16[4,256,256]{2,1,0:T(8,128)(2,1)}), bf16[4,256,256]{2,1,0:T(8,128)(2,1)S(1)}, u32[]{:S(2)}, u32[]{:S(2)}) async-start(bf16[4,256,256]{2,1,0:T(8,128)(2,1)} %tie.15), calls=%async_computation.7 | async-start | bytes 1048576 | tf_op jit(solution)/shard_map/all_to_all | solution.py:544
Sparse Core Ops, SparseCore 0:
  9.9 38.3 all-gather.11
  50.8 65.8 all-gather.5
  140.3 106.6 reduce-scatter.5
  267.1 79.6 reduce-scatter.7
  410.2 77.1 all-gather.9
  488.8 79.2 all-gather.7
  591.0 39.3 reduce-scatter.9

commit v2 on v1

--- a/solution.py
+++ b/solution.py
@@ -451,6 +451,13 @@
             kept.append(lax.ppermute(parts[s], "dp", turn))
         return kept
 
+    def to_planes(parts):
+        twice = jnp.concatenate([parts, parts])
+        return [
+            lax.dynamic_index_in_dim(twice, data_index + s, 0, keepdims=False)
+            for s in range(data_count)
+        ]
+
     def send(which, after=()):
         sending = pack(
             which, int_values, scales[which], bucket_slot[which], quarter, rows_each, after
@@ -469,16 +476,15 @@
     order = jnp.stack([turns, turns ^ 1], axis=1).reshape(own_count)
 
     near = lax.all_gather(out_grad, "own", axis=0, axis_index_groups=likes)
-    far = jnp.stack(exchange([out_grad] * data_count)[1:])
+    far = exchange([out_grad] * data_count)[1:]
+    passed = tuple(mark(part) for part in far)
+    far = jnp.stack(far)
 
     local = inputs.reshape(local_tokens, row_blocks // own_count, data_count, rows_each)
     local = local.transpose(2, 0, 1, 3).reshape(data_count, local_tokens, depth // own_count)
-    twice = jnp.concatenate([local, local])
-    local = exchange(
-        [lax.dynamic_index_in_dim(twice, data_index + s, 0, keepdims=False) for s in range(data_count)]
-    )
+    local = exchange(to_planes(local))
     sending_gate = send(0)
-    local = in_order(local, quarter, (mark(sending_gate), mark(far)))
+    local = in_order(local, quarter, (mark(sending_gate),) + passed)
     gathered = lax.all_gather(local.reshape(tokens, depth // own_count), "own", axis=0)
     sending_up, sending_down = send(1, (mark(local),)), send(2, (mark(local),))
     arrived_gate = receive(sending_gate)

time: 700 us -> 683 us (0.976)
  waiting for transfers between devices: 379 us -> 362 us
    reduce_scatter x1, waiting for transfers between devices: 1.08 us -> 67.7 us  [per_device(): gate = lax.psum_scatter(part, 'dp', scatter_dimension=0)]
    ppermute x6, waiting for transfers between devices: 90.3 us -> 29.3 us  [exchange(): kept.append(lax.ppermute(parts[s], 'dp', turn))]
    ppermute x3, waiting for transfers between devices: 45.6 us -> 25 us  [per_device(): lax.ppermute(far[0], 'own', [(i, i ^ 2 * turn) for i in range(own_count)])]
    all_gather x1, waiting for transfers between devices: 52.5 us -> 40.7 us  [per_device(): lax.all_gather(local.reshape(tokens, depth // own_count), 'own', axis=0)]
    squeeze x16 -> x18, local copies, waits for them, and re-layouts: 19.7 us -> 20.9 us  [mark(): return value.reshape((-1,) + value.shape[-2:])[0, :16, :128]]
  transfers between devices with their start and end apart: 26 -> 26, of which waited for: 16 -> 18; matrix products, arithmetic and copies ran while one was open for 8% -> 9% of each run, Pallas kernels for 22% -> 22%
where the time goes in v2:
time: 683 us; the launch traced here: 681 us
  waiting for transfers between devices  362 us (53%)
  Pallas kernels  184 us (27%)
  starting transfers between devices  48.8 us (7%)
  local copies, waits for them, and re-layouts  47.3 us (7%)
  other arithmetic  23.8 us (3%)
  between operations  14.5 us (2%)
    all_to_all x3, waiting for transfers between devices, give_back(): lax.all_to_all(leaving, 'own', split_axis=0, concat_axis=0, tiled=True)  117 us
    reduce_scatter x1, waiting for transfers between devices, per_device(): gate = lax.psum_scatter(part, 'dp', scatter_dimension=0)  67.7 us
    all_to_all x3, waiting for transfers between devices, receive(): lax.all_to_all(sending, 'own', split_axis=0, concat_axis=0, tiled=True)  49.8 us
    all_gather x1, waiting for transfers between devices, per_device(): lax.all_gather(local.reshape(tokens, depth // own_count), 'own', axis=0)  40.7 us
    pallas_call x2, Pallas kernels, forward(): pl.pallas_call(kernel, out_shape=(jax.ShapeDtypeStruct((row_blocks, rows_...  37.4 us
    pallas_call x2, Pallas kernels, weight_grad(): pl.pallas_call(kernel, out_shape=jax.ShapeDtypeStruct((places, rows_each,...  36 us
    ppermute x6, waiting for transfers between devices, exchange(): kept.append(lax.ppermute(parts[s], 'dp', turn))  29.3 us
    pallas_call x2, Pallas kernels, input_part(): pl.pallas_call(kernel, out_shape=(out, out), grid_spec=pltpu.PrefetchScal...  28.5 us
  transfers between devices with their start and end apart: 26, of which 18 were waited for; matrix products, arithmetic and copies ran while one was open for 9% of the time, Pallas kernels for 22%

profile of v2, /device:TPU:0, one launch (start us, length us, event | category | flops | bytes accessed | tf_op | source)
XLA Modules:
  0.0 680.7 jit_solution(5750624886199029269)
XLA Ops:
  8.0 4.1 collective-permute-start.4
  12.1 1.6 collective-permute-start.3
  13.7 2.2 collective-permute-start.5
  18.9 3.4 reduce-window.6
  22.8 3.6 select_reduce_fusion.1
  27.8 6.2 pack.3
  34.0 1.3 slice_bitcast_fusion.15.refs_4_
  36.1 12.3 %collective-permute-done.4 = bf16[256,1024]{1,0:T(8,128)(2,1)S(1)} collective-permute-done((bf16[256,1024]{1,0:T(8,128)(2,1)}, bf16[256,1024]{1,0:T(8,128)(2,1)S(1)}, u32[]{:S(2)}, u32[]{:S(2)}) %collective-permute-start.4) | collective-permute-done | bytes 524320 | tf_op jit(solution)/shard_map/ppermute | solution.py:451
  49.6 1.8 collective-permute-done.5
  52.0 15.2 %collective-permute-done.1.refs_2_ = bf16[256,256]{1,0:T(8,128)(2,1)S(1)} collective-permute-done((bf16[256,256]{1,0:T(8,128)(2,1)S(1)}, bf16[256,256]{1,0:T(8,128)(2,1)S(1)}, u32[]{:S(2)}, u32[]{:S(2)}) %collective-permute-start.1) | collective-permute-done | bytes 131104 | tf_op jit(solution)/shard_map/ppermute | solution.py:451
  67.9 1.9 in_order.1
  69.9 4.8 all-to-all-start
  78.3 1.3 slice_bitcast_fusion.11.refs_0_
  79.6 6.5 pack.5
  86.1 6.1 pack.4
  92.2 1.3 slice_bitcast_fusion.9
  93.5 1.3 slice_bitcast_fusion.8.refs_2_
  94.7 40.7 %all-gather.6.cloned.1.call-done = bf16[8,1024,256]{2,1,0:T(8,128)(2,1)} async-done(((bf16[1,1024,256]{2,1,0:T(8,128)(2,1)}), bf16[8,1024,256]{2,1,0:T(8,128)(2,1)}) %all-gather.6.cloned.1.call-update) | async-done | bytes 4194320 | tf_op jit(solution)/shard_map/all_gather | solution.py:488
  135.4 4.8 copy.87
  140.2 4.6 all-to-all-done
  144.9 18.7 %forward.2 = (bf16[64,32,2048]{2,1,0:T(8,128)(2,1)}, bf16[4,16,32,1024]{3,2,1,0:T(8,128)(2,1)}) custom-call(s32[416]{0:T(512)} %bitcast.175, s32[416]{0:T(512)} %bitcast.171, bf16[1024,2048]{1,0:T(8,128)(2,1)} %bitcast.125, bf16[560,32,128]{2,1,0:T(8,128)(2,1)} %bitcast.24.arrived, bf16[16,128]{1,0:T(8,128)(2,1)} %get-tuple-element.53.refs_0_, ...), custom_call_target="tpu_custom_call" | custom-call | flops 1024 | bytes 1024 | tf_op jit(solution)/shard_map/forward/pallas_call | solution.py:106
  163.6 1.3 slice_bitcast_fusion.18.refs_1_
  164.9 7.4 %all-to-all-start.1 = ((bf16[8,70,32,128]{3,2,1,0:T(8,128)(2,1)}), bf16[8,70,32,128]{3,2,1,0:T(8,128)(2,1)}, u32[]{:S(2)}, u32[]{:S(2)}) async-start(bf16[8,70,32,128]{3,2,1,0:T(8,128)(2,1)} %tie.9), calls=%async_computation.1 | async-start | bytes 9175040 | tf_op jit(solution)/shard_map/all_to_all | solution.py:468
  172.3 1.3 pad_maximum_fusion.1.refs_0_
  174.9 3.1 collective-permute-start.8
  178.0 1.7 collective-permute-start.7
  179.7 67.7 %reduce-scatter.6.cloned.1.call-done = bf16[1,16,32,1024]{3,2,1,0:T(8,128)(2,1)} async-done(((bf16[4,16,32,1024]{3,2,1,0:T(8,128)(2,1)}), bf16[1,16,32,1024]{3,2,1,0:T(8,128)(2,1)}) %reduce-scatter.6.cloned.1.call-update) | async-done | bytes 1048592 | tf_op jit(solution)/shard_map/reduce_scatter | solution.py:500
  248.6 18.7 %forward.3 = (bf16[64,32,2048]{2,1,0:T(8,128)(2,1)}, bf16[4,16,32,1024]{3,2,1,0:T(8,128)(2,1)}) custom-call(s32[416]{0:T(512)} %bitcast.177, s32[416]{0:T(512)} %bitcast.173, bf16[1024,2048]{1,0:T(8,128)(2,1)} %bitcast.126, bf16[560,32,128]{2,1,0:T(8,128)(2,1)} %bitcast.40.arrived, bf16[16,128]{1,0:T(8,128)(2,1)} %slice_bitcast_fusion.6.refs_0_), custom_call_target="tpu_custom_call" | custom-call | flops 1024 | bytes 1024 | tf_op jit(solution)/shard_map/forward/pallas_call | solution.py:106
  267.4 1.3 slice_bitcast_fusion.17.refs_1_
  268.6 23.4 %collective-permute-done.7.refs_0_ = bf16[3,256,1024]{2,1,0:T(8,128)(2,1)S(1)} collective-permute-done((bf16[3,256,1024]{2,1,0:T(8,128)(2,1)}, bf16[3,256,1024]{2,1,0:T(8,128)(2,1)S(1)}, u32[]{:S(2)}, u32[]{:S(2)}) %collective-permute-start.7) | collective-permute-done | bytes 1572896 | tf_op jit(solution)/shard_map/ppermute | solution.py:494
  292.1 1.5 collective-permute-done.6.refs_0_
  293.6 1.4 copy-done
  296.1 4.3 pad_maximum_fusion.far
  301.6 4.7 all-to-all-start.2
  307.8 6.7 collective-permute-done.9.near_other
  314.5 45.2 %all-to-all-done.2 = bf16[8,70,32,128]{3,2,1,0:T(8,128)(2,1)} async-done(((bf16[8,70,32,128]{3,2,1,0:T(8,128)(2,1)}), bf16[8,70,32,128]{3,2,1,0:T(8,128)(2,1)}, u32[]{:S(2)}, u32[]{:S(2)}) %all-to-all-start.2) | async-done | bytes 4587552 | tf_op jit(solution)/shard_map/all_to_all | solution.py:468
  359.7 24.2 %forward_down.1 = f32[512,1024]{1,0:T(8,128)} custom-call(s32[416]{0:T(512)} %bitcast.169, s32[416]{0:T(512)} %bitcast.167, s32[1]{0:T(128)} %bitcast.3.quarter, s32[8]{0:T(128)} %reshape.193.order, bf16[4,256,1024]{2,1,0:T(8,128)(2,1)} %bitcast.141, bf16[4,3,256,1024]{3,2,1,0:T(8,128)(2,1)} %pad_maximum_fusion.far, ...), custom_call_target="tpu_custom_call" | custom-call | flops 1024 | bytes 1024 | tf_op jit(solution)/shard_map/forward_down/pallas_call | solution.py:170
  383.9 5.1 multiply_convert_fusion
  389.0 20.9 %weight_grad_down.1 = bf16[560,32,128]{2,1,0:T(8,128)(2,1)} custom-call(s32[416]{0:T(512)} %bitcast.170, s32[416]{0:T(512)} %bitcast.168, s32[1]{0:T(128)} %bitcast.3.quarter, s32[8]{0:T(128)} %reshape.193.order, bf16[512,1024]{1,0:T(8,128)(2,1)} %get-tuple-element.30.value, bf16[4,256,1024]{2,1,0:T(8,128)(2,1)} %bitcast.142, ...), custom_call_target="tpu_custom_call" | custom-call | flops 1024 | bytes 1024 | tf_op jit(solution)/shard_map/weight_grad_down/pallas_call | solution.py:272
  410.0 4.6 all-to-all-start.3
  415.1 6.5 copy.81
  421.6 46.3 %all-to-all-done.3 = bf16[8,70,32,128]{3,2,1,0:T(8,128)(2,1)} async-done(((bf16[8,70,32,128]{3,2,1,0:T(8,128)(2,1)}), bf16[8,70,32,128]{3,2,1,0:T(8,128)(2,1)}, u32[]{:S(2)}, u32[]{:S(2)}) %all-to-all-start.3) | async-done | bytes 4587552 | tf_op jit(solution)/shard_map/all_to_all | solution.py:519
  469.2 2.0 all-gather.10.cloned.1.call-done.grad
  471.1 18.0 %weight_grad.2 = bf16[560,32,128]{2,1,0:T(8,128)(2,1)} custom-call(s32[416]{0:T(512)} %bitcast.178, s32[416]{0:T(512)} %bitcast.174, bf16[2048,1024]{1,0:T(8,128)(2,1)} %bitcast.127, bf16[4,16,32,1024]{3,2,1,0:T(8,128)(2,1)} %all-gather.10.cloned.1.call-done.grad, bf16[16,128]{1,0:T(8,128)(2,1)} %slice_bitcast_fusion.4.refs_0_), custom_call_target="tpu_custom_call" | custom-call | flops 1024 | bytes 1024 | tf_op jit(solution)/shard_map/weight_grad/pallas_call | solution.py:210
  489.2 4.6 all-to-all-start.4
  495.9 5.5 unpack.3.refs_0_
  501.4 1.3 slice_bitcast_fusion.1.refs_3_
  502.7 1.3 slice_bitcast_fusion.3.refs_0_
  503.9 13.9 %input_part.2 = (f32[4,256,1024]{2,1,0:T(8,128)}, f32[4,256,1024]{2,1,0:T(8,128)}) custom-call(s32[1]{0:T(128)} %bitcast.first, bf16[2048,2048]{1,0:T(8,128)(2,1)} %bitcast.131, bf16[2048,2048]{1,0:T(8,128)(2,1)} %bitcast.132, bf16[4,16,32,1024]{3,2,1,0:T(8,128)(2,1)} %all-gather.10.cloned.1.call-done.grad, bf16[16,128]{1,0:T(8,128)(2,1)} %slice_bitcast_fusion.3.refs_0_), custom_call_target="tpu_custom_call" | custom-call | flops 1024 | bytes 1024 | tf_op jit(solution)/shard_map/input_part/pallas_call | solution.py:317
  517.8 29.3 %all-to-all-done.4 = bf16[8,70,32,128]{3,2,1,0:T(8,128)(2,1)} async-done(((bf16[8,70,32,128]{3,2,1,0:T(8,128)(2,1)}), bf16[8,70,32,128]{3,2,1,0:T(8,128)(2,1)}, u32[]{:S(2)}, u32[]{:S(2)}) %all-to-all-start.4) | async-done | bytes 4587552 | tf_op jit(solution)/shard_map/all_to_all | solution.py:519
  548.4 3.5 all-gather.8.cloned.1.call-done.grad
  551.9 14.6 %input_part.3 = (bf16[4,256,1024]{2,1,0:T(8,128)(2,1)}, bf16[4,256,1024]{2,1,0:T(8,128)(2,1)}) custom-call(s32[1]{0:T(128)} %bitcast.first, bf16[2048,2048]{1,0:T(8,128)(2,1)} %bitcast.129, bf16[2048,2048]{1,0:T(8,128)(2,1)} %bitcast.130, bf16[4,16,32,1024]{3,2,1,0:T(8,128)(2,1)} %all-gather.8.cloned.1.call-done.grad, ...), custom_call_target="tpu_custom_call" | custom-call | flops 1024 | bytes 1024 | tf_op jit(solution)/shard_map/input_part/pallas_call | solution.py:317
  566.4 4.4 collective-permute-done.11
  570.8 3.9 add_convert_fusion
  574.7 1.3 slice_bitcast_fusion.16.refs_0_
  576.0 17.9 %weight_grad.3 = bf16[560,32,128]{2,1,0:T(8,128)(2,1)} custom-call(s32[416]{0:T(512)} %bitcast.176, s32[416]{0:T(512)} %bitcast.172, bf16[2048,1024]{1,0:T(8,128)(2,1)} %bitcast.128, bf16[4,16,32,1024]{3,2,1,0:T(8,128)(2,1)} %all-gather.8.cloned.1.call-done.grad, bf16[16,128]{1,0:T(8,128)(2,1)} %slice_bitcast_fusion.16.refs_0_), custom_call_target="tpu_custom_call" | custom-call | flops 1024 | bytes 1024 | tf_op jit(solution)/shard_map/weight_grad/pallas_call | solution.py:210
  593.9 4.6 all-to-all-start.6
  598.5 5.6 unpack.4.refs_0_
  604.1 1.3 slice_bitcast_fusion.refs_1_
  605.3 8.9 %reduce-scatter.10.cloned.1.call-done = bf16[1,256,1024]{2,1,0:T(8,128)(2,1)} async-done(((bf16[4,256,1024]{2,1,0:T(8,128)(2,1)}), bf16[1,256,1024]{2,1,0:T(8,128)(2,1)}) %reduce-scatter.10.cloned.1.call-update) | async-done | bytes 524304
  616.4 41.0 %all-to-all-done.6 = bf16[8,70,32,128]{3,2,1,0:T(8,128)(2,1)} async-done(((bf16[8,70,32,128]{3,2,1,0:T(8,128)(2,1)}), bf16[8,70,32,128]{3,2,1,0:T(8,128)(2,1)}, u32[]{:S(2)}, u32[]{:S(2)}) %all-to-all-start.6) | async-done | bytes 4587552 | tf_op jit(solution)/shard_map/all_to_all | solution.py:519
  657.5 3.5 all-to-all-start.5
  660.9 5.4 unpack.5
  666.4 6.4 all-to-all-done.5
  (121 shorter events, 27.3 us)
Async XLA Ops:
  7.2 11.2 %copy-start.11 = (s32[3,128,26]{1,2,0:T(8,128)S(1)}, s32[3,128,26]{1,2,0:T(8,128)}, u32[]{:S(2)}) copy-start(s32[3,128,26]{1,2,0:T(8,128)} %param.13) | copy-start | bytes 119812
  7.2 11.4 %copy-start.7 = (s32[3,128,26]{1,2,0:T(8,128)S(1)}, s32[3,128,26]{1,2,0:T(8,128)}, u32[]{:S(2)}) copy-start(s32[3,128,26]{1,2,0:T(8,128)} %param.12) | copy-start | bytes 119812
  7.2 19.3 %copy-start.13 = (f32[3,416]{1,0:T(4,128)S(1)}, f32[3,416]{1,0:T(4,128)}, u32[]{:S(2)}) copy-start(f32[3,416]{1,0:T(4,128)} %param.10) | copy-start | bytes 14980
  7.2 86.3 %all-gather.12.cloned.1.call-start = ((), (), s32[]{:S(2)}) async-start(), calls=%async_computation.15 | async-start | bytes 2621440 | tf_op jit(solution)/shard_map/all_gather | solution.py:478
  7.9 127.5 %all-gather.6.cloned.1.call-start = ((), (), s32[]{:S(2)}) async-start(), calls=%async_computation.10 | async-start | bytes 4718592 | tf_op jit(solution)/shard_map/all_gather | solution.py:488
  8.0 40.4 %collective-permute-start.4 = (bf16[256,1024]{1,0:T(8,128)(2,1)}, bf16[256,1024]{1,0:T(8,128)(2,1)S(1)}, u32[]{:S(2)}, u32[]{:S(2)}) collective-permute-start(bf16[256,1024]{1,0:T(8,128)(2,1)} %param.8), channel_id=1, source_target_pairs={{0,16},{8,24},{16,0},{24,8},{1,17},{9,25},{17,1},{25,9},{2,18},{10... | collective-permute-start | bytes 1572872 | tf_op jit(solution)/shard_map/ppermute | solution.py:451
  12.1 36.9 %collective-permute-start.3 = (bf16[256,1024]{1,0:T(8,128)(2,1)}, bf16[256,1024]{1,0:T(8,128)(2,1)S(1)}, u32[]{:S(2)}, u32[]{:S(2)}) collective-permute-start(bf16[256,1024]{1,0:T(8,128)(2,1)} %param.8), channel_id=1, source_target_pairs={{0,8},{8,16},{16,24},{24,0},{1,9},{9,17},{17,25},{25,1},{2,10},{10... | collective-permute-start | bytes 1572872 | tf_op jit(solution)/shard_map/ppermute | solution.py:451
  13.7 37.7 %collective-permute-start.5 = (bf16[256,1024]{1,0:T(8,128)(2,1)}, bf16[256,1024]{1,0:T(8,128)(2,1)S(1)}, u32[]{:S(2)}, u32[]{:S(2)}) collective-permute-start(bf16[256,1024]{1,0:T(8,128)(2,1)} %param.8), channel_id=1, source_target_pairs={{0,24},{8,0},{16,8},{24,16},{1,25},{9,1},{17,9},{25,17},{2,26},{10... | collective-permute-start | bytes 1572872 | tf_op jit(solution)/shard_map/ppermute | solution.py:451
  17.5 34.5 %collective-permute-start = (bf16[256,256]{1,0:T(8,128)(2,1)S(1)}, bf16[256,256]{1,0:T(8,128)(2,1)S(1)}, u32[]{:S(2)}, u32[]{:S(2)}) collective-permute-start(bf16[256,256]{1,0:T(8,128)(2,1)S(1)} %bitcast.163), channel_id=1, source_target_pairs={{0,8},{8,16},{16,24},{24,0},{1,9},{9,17},{17,25},{25,1},{2,10},{10... | collective-permute-start | bytes 393224 | tf_op jit(solution)/shard_map/ppermute | solution.py:451
  17.7 49.5 %collective-permute-start.1 = (bf16[256,256]{1,0:T(8,128)(2,1)S(1)}, bf16[256,256]{1,0:T(8,128)(2,1)S(1)}, u32[]{:S(2)}, u32[]{:S(2)}) collective-permute-start(bf16[256,256]{1,0:T(8,128)(2,1)S(1)} %bitcast.164), channel_id=1, source_target_pairs={{0,16},{8,24},{16,0},{24,8},{1,17},{9,25},{17,1},{25,9},{2,18},{10... | collective-permute-start | bytes 393224 | tf_op jit(solution)/shard_map/ppermute | solution.py:451
  48.4 18.8 %collective-permute-start.2 = (bf16[256,256]{1,0:T(8,128)(2,1)S(1)}, bf16[256,256]{1,0:T(8,128)(2,1)S(1)}, u32[]{:S(2)}, u32[]{:S(2)}) collective-permute-start(bf16[256,256]{1,0:T(8,128)(2,1)S(1)} %bitcast.165), channel_id=1, source_target_pairs={{0,24},{8,0},{16,8},{24,16},{1,25},{9,1},{17,9},{25,17},{2,26},{10... | collective-permute-start | bytes 393224 | tf_op jit(solution)/shard_map/ppermute | solution.py:451
  52.0 15.2 %copy-start.8 = (bf16[256,256]{1,0:T(8,128)(2,1)}, bf16[256,256]{1,0:T(8,128)(2,1)S(1)}, u32[]{:S(2)}) copy-start(bf16[256,256]{1,0:T(8,128)(2,1)S(1)} %collective-permute-done.refs_1_) | copy-start | bytes 393220
  67.2 0.7 copy-start.9
  67.2 0.7 copy-start.10
  69.9 4.9 copy-start.12
  69.9 75.0 %all-to-all-start = ((bf16[8,70,32,128]{3,2,1,0:T(8,128)(2,1)}), bf16[8,70,32,128]{3,2,1,0:T(8,128)(2,1)}, u32[]{:S(2)}, u32[]{:S(2)}) async-start(bf16[8,70,32,128]{3,2,1,0:T(8,128)(2,1)} %bitcast.134), calls=%async_computation | async-start | bytes 9175040 | tf_op jit(solution)/shard_map/all_to_all | solution.py:468
  74.7 172.7 %reduce-scatter.6.cloned.1.call-start = ((), (), s32[]{:S(2)}) async-start(), calls=%async_computation.11 | async-start | bytes 5242880 | tf_op jit(solution)/shard_map/reduce_scatter | solution.py:500
  164.9 83.8 %all-to-all-start.1 = ((bf16[8,70,32,128]{3,2,1,0:T(8,128)(2,1)}), bf16[8,70,32,128]{3,2,1,0:T(8,128)(2,1)}, u32[]{:S(2)}, u32[]{:S(2)}) async-start(bf16[8,70,32,128]{3,2,1,0:T(8,128)(2,1)} %tie.9), calls=%async_computation.1 | async-start | bytes 9175040 | tf_op jit(solution)/shard_map/all_to_all | solution.py:468
  172.3 211.6 %reduce-scatter.8.cloned.1.call-start = ((), (), s32[]{:S(2)}) async-start(), calls=%async_computation.12 | async-start | bytes 5242880 | tf_op jit(solution)/shard_map/reduce_scatter | solution.py:505
  174.9 93.7 %collective-permute-start.8 = (bf16[3,256,1024]{2,1,0:T(8,128)(2,1)}, bf16[3,256,1024]{2,1,0:T(8,128)(2,1)S(1)}, u32[]{:S(2)}, u32[]{:S(2)}) collective-permute-start(bf16[3,256,1024]{2,1,0:T(8,128)(2,1)} %tie.8.refs_0_), channel_id=1, source_target_pairs={{0,6},{1,7},{2,4},{3,5},{4,2},{5,3},{6,0},{7,1},{8,14},{9,15},{10,... | collective-permute-start | bytes 4718600 | tf_op jit(solution)/shard_map/ppermute | solution.py:494
  178.0 114.1 %collective-permute-start.7 = (bf16[3,256,1024]{2,1,0:T(8,128)(2,1)}, bf16[3,256,1024]{2,1,0:T(8,128)(2,1)S(1)}, u32[]{:S(2)}, u32[]{:S(2)}) collective-permute-start(bf16[3,256,1024]{2,1,0:T(8,128)(2,1)} %tie.8.refs_0_), channel_id=1, source_target_pairs={{0,4},{1,5},{2,6},{3,7},{4,0},{5,1},{6,2},{7,3},{8,12},{9,13},{10,... | collective-permute-start | bytes 4718600 | tf_op jit(solution)/shard_map/ppermute | solution.py:494
  179.7 113.9 %collective-permute-start.6 = (bf16[3,256,1024]{2,1,0:T(8,128)(2,1)}, bf16[3,256,1024]{2,1,0:T(8,128)(2,1)}, u32[]{:S(2)}, u32[]{:S(2)}) collective-permute-start(bf16[3,256,1024]{2,1,0:T(8,128)(2,1)} %tie.8.refs_0_), channel_id=1, source_target_pairs={{0,2},{1,3},{2,0},{3,1},{4,6},{5,7},{6,4},{7,5},{8,10},{9,11},{10,... | collective-permute-start | bytes 4718600 | tf_op jit(solution)/shard_map/ppermute | solution.py:494
  268.6 25.0 %copy-start.2 = (bf16[3,256,1024]{2,1,0:T(8,128)(2,1)}, bf16[3,256,1024]{2,1,0:T(8,128)(2,1)S(1)}, u32[]{:S(2)}) copy-start(bf16[3,256,1024]{2,1,0:T(8,128)(2,1)S(1)} %collective-permute-done.8.refs_0_) | copy-start | bytes 4718596
  292.1 1.5 copy-start.4
  293.6 1.5 copy-start
  293.6 2.0 copy-start.3
  293.6 2.4 copy-start.5
  300.4 59.3 %collective-permute-start.10 = (bf16[4,3,256,1024]{3,2,1,0:T(8,128)(2,1)}, bf16[4,3,256,1024]{3,2,1,0:T(8,128)(2,1)}, u32[]{:S(2)}, u32[]{:S(2)}) collective-permute-start(bf16[4,3,256,1024]{3,2,1,0:T(8,128)(2,1)} %pad_maximum_fusion.far), channel_id=1, source_target_pairs={{0,1},{1,0},{2,3},{3,2},{4,5},{5,4},{6,7},{7,6},{8,9},{9,8},{10,11... | collective-permute-start | bytes 18874376 | tf_op jit(solution)/shard_map/ppermute | solution.py:507
  301.6 4.9 copy-start.1
  301.6 58.0 %all-to-all-start.2 = ((bf16[8,70,32,128]{3,2,1,0:T(8,128)(2,1)}), bf16[8,70,32,128]{3,2,1,0:T(8,128)(2,1)}, u32[]{:S(2)}, u32[]{:S(2)}) async-start(bf16[8,70,32,128]{3,2,1,0:T(8,128)(2,1)} %tie.14), calls=%async_computation.3 | async-start | bytes 9175040 | tf_op jit(solution)/shard_map/all_to_all | solution.py:468
  306.3 164.8 %all-gather.10.cloned.1.call-start = ((), (), s32[]{:S(2)}) async-start(), calls=%async_computation.14 | async-start | bytes 5242880 | tf_op jit(solution)/shard_map/all_gather | solution.py:522
  306.6 7.9 %collective-permute-start.9 = (bf16[4,256,1024]{2,1,0:T(8,128)(2,1)S(1)}, bf16[4,256,1024]{2,1,0:T(8,128)(2,1)}, u32[]{:S(2)}, u32[]{:S(2)}) collective-permute-start(bf16[4,256,1024]{2,1,0:T(8,128)(2,1)S(1)} %bitcast.143), channel_id=1, source_target_pairs={{0,1},{1,0},{2,3},{3,2},{4,5},{5,4},{6,7},{7,6},{8,9},{9,8},{10,11... | collective-permute-start | bytes 6291464 | tf_op jit(solution)/shard_map/ppermute | solution.py:507
  359.7 24.2 %copy-start.6 = (bf16[1,16,32,1024]{3,2,1,0:T(8,128)(2,1)S(1)}, bf16[1,16,32,1024]{3,2,1,0:T(8,128)(2,1)}, u32[]{:S(2)}) copy-start(bf16[1,16,32,1024]{3,2,1,0:T(8,128)(2,1)} %reduce-scatter.6.cloned.1.call-done) | copy-start | bytes 3145732
  410.0 57.9 %all-to-all-start.3 = ((bf16[8,70,32,128]{3,2,1,0:T(8,128)(2,1)}), bf16[8,70,32,128]{3,2,1,0:T(8,128)(2,1)}, u32[]{:S(2)}, u32[]{:S(2)}) async-start(bf16[8,70,32,128]{3,2,1,0:T(8,128)(2,1)} %bitcast.136), calls=%async_computation.5 | async-start | bytes 9175040 | tf_op jit(solution)/shard_map/all_to_all | solution.py:519
  414.6 137.3 %all-gather.8.cloned.1.call-start = ((), (), s32[]{:S(2)}) async-start(), calls=%async_computation.13 | async-start | bytes 5242880 | tf_op jit(solution)/shard_map/all_gather | solution.py:526
  489.2 57.9 %all-to-all-start.4 = ((bf16[8,70,32,128]{3,2,1,0:T(8,128)(2,1)}), bf16[8,70,32,128]{3,2,1,0:T(8,128)(2,1)}, u32[]{:S(2)}, u32[]{:S(2)}) async-start(bf16[8,70,32,128]{3,2,1,0:T(8,128)(2,1)} %bitcast.135), calls=%async_computation.6 | async-start | bytes 9175040 | tf_op jit(solution)/shard_map/all_to_all | solution.py:519
  493.8 120.4 %reduce-scatter.10.cloned.1.call-start = ((), (), s32[]{:S(2)}) async-start(), calls=%async_computation.16 | async-start | bytes 2621440
  566.4 4.4 collective-permute-start.11
  593.9 63.6 %all-to-all-start.6 = ((bf16[8,70,32,128]{3,2,1,0:T(8,128)(2,1)}), bf16[8,70,32,128]{3,2,1,0:T(8,128)(2,1)}, u32[]{:S(2)}, u32[]{:S(2)}) async-start(bf16[8,70,32,128]{3,2,1,0:T(8,128)(2,1)} %bitcast.137), calls=%async_computation.8 | async-start | bytes 9175040 | tf_op jit(solution)/shard_map/all_to_all | solution.py:519
  657.5 15.4 %all-to-all-start.5 = ((bf16[4,256,256]{2,1,0:T(8,128)(2,1)}), bf16[4,256,256]{2,1,0:T(8,128)(2,1)S(1)}, u32[]{:S(2)}, u32[]{:S(2)}) async-start(bf16[4,256,256]{2,1,0:T(8,128)(2,1)} %tie.15), calls=%async_computation.7 | async-start | bytes 1048576 | tf_op jit(solution)/shard_map/all_to_all | solution.py:550
Sparse Core Ops, SparseCore 0:
  9.9 38.0 all-gather.11
  70.0 65.3 all-gather.5
  163.7 83.6 reduce-scatter.5
  267.5 77.2 reduce-scatter.7
  389.1 81.9 all-gather.9
  472.6 79.2 all-gather.7
  574.8 39.3 reduce-scatter.9
